TPU v7x, 128 devices: a whole 4x4x4 slice. The times are simulated.
128 devices in a mesh: seq: 16 (over z, x), vis: 8 (over y, core).
Axes of the slice: x: 4, y: 4, z: 4, core: 2. Of those that a mesh axis runs over, the one named last changes fastest.
Arguments:
- query: bfloat16 [5120, 4096], P('seq', 'vis'), may hold values from -15 to 15
- key: bfloat16 [5120, 4096], P('seq', 'vis'), may hold values from -15 to 15
- value: bfloat16 [5120, 4096], P('seq', 'vis'), may hold values from -6 to 6
- doc_ids: int32 [5120], P('seq'), may hold values from 0 to 3, never falling along the last dimension, each value on 1 to 2560 neighbouring positions
- cross_query: bfloat16 [5120, 4096], P('seq', 'vis'), may hold values from -15 to 15
- latent_key: bfloat16 [8, 64, 4096], P('vis'), may hold values from -15 to 15
- latent_value: bfloat16 [8, 64, 4096], P('vis'), may hold values from -6 to 6
- token_slot: int32 [5120], P('seq'), may hold values from 0 to 4, as said below
- slot_image: int32 [64], P('seq'), may hold values from 0 to 7, as said below
- cross_gate: float32 [4096], P('vis'), may hold values from -1.5 to 1.5
- out_grad: bfloat16 [5120, 4096], P('seq', 'vis'), may hold values from -6 to 6
Outputs:
- mixed: bfloat16 [5120, 4096], P('seq', 'vis')
- query_grad: float32 [5120, 4096], P('seq', 'vis')
- key_grad: float32 [5120, 4096], P('seq', 'vis')
- value_grad: float32 [5120, 4096], P('seq', 'vis')
- cross_query_grad: float32 [5120, 4096], P('seq', 'vis')
- latent_key_grad: float32 [8, 64, 4096], P('vis', None, 'seq')
- latent_value_grad: float32 [8, 64, 4096], P('vis', None, 'seq')
Inputs may be any that keep to these rules, and one draw needn't show every extreme that they name: `token_slot`: within each text shard of 320 tokens the values after the leading 4s never fall; 4 marks the tokens before the shard's first image, which see no image. `slot_image`: the images of one shard's slots need not differ; image m is held by index m of vis.
All inputs are finite; a program needn't handle non-finite values.
Results may differ from a plain program's by a relative error of at most 0.03.
Values may be sent and summed in bfloat16 or wider, within the bound.
A program may use at most 192 MiB of HBM per device.

v0:
```python
import math

import jax
import jax.numpy as jnp
from jax import lax
from jax.sharding import PartitionSpec as P

HEAD_DIM = 128


big_negative = -1e30


def pair_scores(left, right):
    return jnp.einsum("id,jd->ij", left, right, preferred_element_type=jnp.float32)


def softmax_rows(scores, allowed):
    masked = jnp.where(allowed, scores, big_negative)
    row_max = jnp.max(masked, axis=1)
    weights = jnp.where(allowed, jnp.exp(masked - row_max[:, None]), 0.0)
    return (weights, row_max, jnp.sum(weights, axis=1))


def shards(
    query,
    key,
    value,
    doc_ids,
    cross_query,
    latent_key,
    latent_value,
    token_slot,
    slot_image,
    cross_gate,
    out_grad,
):
    row_count, width_dev = query.shape
    head_count = width_dev // HEAD_DIM
    score_scale = 1.0 / math.sqrt(HEAD_DIM)
    seq_index = lax.axis_index("seq")
    vis_index = lax.axis_index("vis")
    keys_all, values_all, docs_all = (
        lax.all_gather(key, "seq", axis=0, tiled=True),
        lax.all_gather(value, "seq", axis=0, tiled=True),
        lax.all_gather(doc_ids, "seq", axis=0, tiled=True),
    )
    key_count = keys_all.shape[0]
    query_pos = seq_index * row_count + jnp.arange(row_count, dtype=jnp.int32)
    key_pos = jnp.arange(key_count, dtype=jnp.int32)
    allowed = (key_pos[None, :] <= query_pos[:, None]) & (docs_all[None, :] == doc_ids[:, None])
    slot_count = slot_image.shape[0]
    latent_count = latent_key.shape[1]
    image_local = latent_key.shape[0]
    owner_index = slot_image // image_local
    local_slot = jnp.clip(slot_image - owner_index * image_local, 0, image_local - 1)
    owned = (owner_index == vis_index)[:, None, None]
    picked_key = jnp.where(owned, jnp.take(latent_key, local_slot, axis=0).astype(jnp.float32), 0.0)
    picked_value = jnp.where(
        owned, jnp.take(latent_value, local_slot, axis=0).astype(jnp.float32), 0.0
    )
    summed_key, summed_value = (
        lax.psum_scatter(
            picked_key.astype(jnp.bfloat16), "vis", scatter_dimension=2, tiled=True
        ).astype(jnp.float32),
        lax.psum_scatter(
            picked_value.astype(jnp.bfloat16), "vis", scatter_dimension=2, tiled=True
        ).astype(jnp.float32),
    )
    slot_key = summed_key.astype(jnp.bfloat16)
    slot_value = summed_value.astype(jnp.bfloat16)
    cross_keys = slot_key.reshape(slot_count * latent_count, width_dev)
    cross_values = slot_value.reshape(slot_count * latent_count, width_dev)
    column_slot = jnp.arange(slot_count * latent_count, dtype=jnp.int32) // latent_count
    cross_allowed = column_slot[None, :] == token_slot[:, None]
    has_image = token_slot < slot_count
    gate_tanh = jnp.tanh(cross_gate)
    mixed_parts, query_parts, cross_parts = ([], [], [])
    key_terms, value_terms = ([], [])
    slot_key_parts, slot_value_parts = ([], [])
    for head_index in range(head_count):
        columns = slice(head_index * HEAD_DIM, (head_index + 1) * HEAD_DIM)
        query_head = query[:, columns]
        key_head = keys_all[:, columns]
        value_head = values_all[:, columns]
        grad_head = out_grad[:, columns]
        scores = pair_scores(query_head, key_head) * score_scale
        weights, row_max, row_total = softmax_rows(scores, allowed)
        probs = weights / row_total[:, None]
        probs_low = probs.astype(jnp.bfloat16)
        self_out = jnp.dot(probs_low, value_head, preferred_element_type=jnp.float32)
        row_dot = jnp.sum(grad_head.astype(jnp.float32) * self_out, axis=1)
        grad_probs = pair_scores(grad_head, value_head)
        grad_scores = (probs * (grad_probs - row_dot[:, None]) * score_scale).astype(jnp.bfloat16)
        query_parts.append(jnp.dot(grad_scores, key_head, preferred_element_type=jnp.float32))
        key_terms.append(
            jnp.einsum("ij,id->jd", grad_scores, query_head, preferred_element_type=jnp.float32)
        )
        value_terms.append(
            jnp.einsum("ij,id->jd", probs_low, grad_head, preferred_element_type=jnp.float32)
        )
        cross_head = cross_query[:, columns]
        cross_key_head = cross_keys[:, columns]
        cross_value_head = cross_values[:, columns]
        cross_scores = pair_scores(cross_head, cross_key_head) * score_scale
        cross_weights, cross_max, cross_total = softmax_rows(cross_scores, cross_allowed)
        cross_probs = cross_weights / jnp.where(has_image, cross_total, 1.0)[:, None]
        cross_low = cross_probs.astype(jnp.bfloat16)
        cross_out = jnp.dot(cross_low, cross_value_head, preferred_element_type=jnp.float32)
        gate_head = gate_tanh[columns]
        mixed_parts.append(self_out + gate_head[None, :] * cross_out)
        cross_back = (gate_head[None, :] * grad_head.astype(jnp.float32)).astype(jnp.bfloat16)
        cross_dot = jnp.sum(cross_back.astype(jnp.float32) * cross_out, axis=1)
        cross_grad_probs = pair_scores(cross_back, cross_value_head)
        cross_grad_scores = (
            cross_probs * (cross_grad_probs - cross_dot[:, None]) * score_scale
        ).astype(jnp.bfloat16)
        cross_parts.append(
            jnp.dot(cross_grad_scores, cross_key_head, preferred_element_type=jnp.float32)
        )
        slot_key_parts.append(
            jnp.einsum(
                "ij,id->jd", cross_grad_scores, cross_head, preferred_element_type=jnp.float32
            ).astype(jnp.bfloat16)
        )
        slot_value_parts.append(
            jnp.einsum(
                "ij,id->jd", cross_low, cross_back, preferred_element_type=jnp.float32
            ).astype(jnp.bfloat16)
        )
    mixed = jnp.concatenate(mixed_parts, axis=1).astype(jnp.bfloat16)
    query_grad = jnp.concatenate(query_parts, axis=1)
    cross_query_grad = jnp.concatenate(cross_parts, axis=1)
    key_grad, value_grad = (
        lax.psum_scatter(
            jnp.concatenate(key_terms, axis=1), "seq", scatter_dimension=0, tiled=True
        ),
        lax.psum_scatter(
            jnp.concatenate(value_terms, axis=1), "seq", scatter_dimension=0, tiled=True
        ),
    )
    slot_key_grad = jnp.concatenate(slot_key_parts, axis=1).reshape(
        slot_count, latent_count, width_dev
    )
    slot_value_grad = jnp.concatenate(slot_value_parts, axis=1).reshape(
        slot_count, latent_count, width_dev
    )
    full_key, full_value = (
        lax.all_gather(slot_key_grad, "vis", axis=2, tiled=True),
        lax.all_gather(slot_value_grad, "vis", axis=2, tiled=True),
    )
    owner_index = slot_image // image_local
    onehot = (
        (slot_image - owner_index * image_local)[None, :]
        == jnp.arange(image_local, dtype=jnp.int32)[:, None]
    ) & (owner_index == vis_index)[None, :]
    onehot = onehot.astype(jnp.bfloat16)
    image_key = jnp.einsum("is,slw->ilw", onehot, full_key, preferred_element_type=jnp.float32)
    image_value = jnp.einsum("is,slw->ilw", onehot, full_value, preferred_element_type=jnp.float32)
    latent_key_grad, latent_value_grad = (
        lax.psum_scatter(
            image_key.astype(jnp.bfloat16), "seq", scatter_dimension=2, tiled=True
        ).astype(jnp.float32),
        lax.psum_scatter(
            image_value.astype(jnp.bfloat16), "seq", scatter_dimension=2, tiled=True
        ).astype(jnp.float32),
    )
    return (
        mixed,
        query_grad,
        key_grad,
        value_grad,
        cross_query_grad,
        latent_key_grad,
        latent_value_grad,
    )


def solution(mesh):
    placed = (
        P("seq", "vis"),
        P("seq", "vis"),
        P("seq", "vis"),
        P("seq"),
        P("seq", "vis"),
        P("vis", None, None),
        P("vis", None, None),
        P("seq"),
        P("seq"),
        P("vis"),
        P("seq", "vis"),
    )
    return jax.shard_map(
        shards,
        mesh=mesh,
        in_specs=placed,
        out_specs=(
            P("seq", "vis"),
            P("seq", "vis"),
            P("seq", "vis"),
            P("seq", "vis"),
            P("seq", "vis"),
            P("vis", None, "seq"),
            P("vis", None, "seq"),
        ),
        check_vma=False,
    )
```

profile of v0, /device:TPU:59, one launch (start us, length us, event | category | flops | bytes accessed | tf_op | source)
XLA Modules:
  0.0 530.0 jit_solution(4862426126979491999)
XLA Ops:
  8.8 4.0 select_convert_fusion
  16.4 52.4 %all-reduce = s32[5120]{0:T(1024)S(1)} all-reduce(s32[5120]{0:T(1024)S(1)} %dynamic-update-slice), channel_id=1, replica_groups=mesh['seq'=16,'vis'=8] {'seq'}, use_global_device_ids=true, to_apply=%add | all-reduce | flops 5120 | bytes 40960
  76.4 5.4 %reduce-scatter.13.cloned.1.call-done = bf16[4,64,512]{2,1,0:T(8,128)(2,1)} async-done(((bf16[4,64,4096]{2,1,0:T(8,128)(2,1)}), bf16[4,64,512]{2,1,0:T(8,128)(2,1)}) %reduce-scatter.13.cloned.1.call-update) | async-done | bytes 262160 | tf_op jit(solution)/shard_map/reduce_scatter | solution.py:66
  85.4 3.6 fusion.186
  93.1 4.7 fusion.189
  97.8 10.5 %fusion.18 = (f32[320]{0:T(512)S(1)}, f32[320]{0:T(512)S(1)}, f32[320]{0:T(512)S(1)}, f32[320]{0:T(512)S(1)}) fusion(f32[320,5120]{1,0:T(8,128)S(1)} %get-tuple-element.77, f32[320]{0:T(512)S(1)} %get-tuple-element.76, s32[320]{0:T(512)S(1)} %copy-done.22, s32[5120]{0:T(1024)S(1)} %all-reduce, s32[320]{0:T(512)S(1)} %iota_add_fusion, ...), kind=kLoop, calls=%fused_computation.33 | loop fusion | flops 24574720 | bytes 26247680 | tf_op jit(solution)/shard_map/reduce_sum | solution.py:22
  108.3 12.3 %fusion.17 = (f32[320,5120]{1,0:T(8,128)}, f32[320,5120]{1,0:T(8,128)}, f32[320,5120]{1,0:T(8,128)}, f32[320,5120]{1,0:T(8,128)}) fusion(f32[320,5120]{1,0:T(8,128)S(1)} %get-tuple-element.77, f32[320]{0:T(512)S(1)} %get-tuple-element.36, f32[320]{0:T(512)S(1)} %get-tuple-element.76, s32[320]{0:T(512)S(1)} %copy-done.22, s32[5120]{0:T(1024)S(1)} %all-reduce, ...), kind=kLoop, calls=%fused_computation.32 | loop fusion | flops 24576000 | bytes 52462080 | tf_op jit(solution)/shard_map/div | solution.py:89
  120.6 10.6 %all-gather.7.cloned.1.call-done = bf16[5120,512]{1,0:T(8,128)(2,1)} async-done(((bf16[320,512]{1,0:T(8,128)(2,1)}), bf16[5120,512]{1,0:T(8,128)(2,1)}) %all-gather.7.cloned.1.call-update) | async-done | bytes 5242896 | tf_op jit(solution)/shard_map/all_gather | solution.py:45
  131.2 4.3 fusion.43
  147.0 11.9 %all-gather.11.cloned.1.call-done = bf16[4,64,4096]{2,1,0:T(8,128)(2,1)} async-done(((bf16[4,64,512]{2,1,0:T(8,128)(2,1)}), bf16[4,64,4096]{2,1,0:T(8,128)(2,1)}) %all-gather.11.cloned.1.call-update) | async-done | bytes 2097168 | tf_op jit(solution)/shard_map/all_gather | solution.py:150
  158.9 3.5 fusion.25
  163.8 4.4 fusion.12
  183.0 3.8 all-gather.9.cloned.1.call-done
  186.8 3.5 fusion.27
  195.3 4.4 pad_maximum_fusion
  199.7 11.4 %copy.32 = f32[5120,512]{1,0:T(8,128)} copy(f32[5120,512]{0,1:T(8,128)} %pad_maximum_fusion) | data formatting | bytes 20971520
  212.1 3.9 fusion.29
  216.0 4.0 fusion.33
  222.8 4.5 pad_maximum_fusion.1
  227.3 11.4 %copy.34 = f32[5120,512]{1,0:T(8,128)} copy(f32[5120,512]{0,1:T(8,128)} %pad_maximum_fusion.1) | data formatting | bytes 20971520
  238.8 21.8 %reduce-scatter.17.cloned.1.call-done = bf16[1,64,256]{2,1,0:T(8,128)(2,1)} async-done(((bf16[1,64,4096]{2,1,0:T(8,128)(2,1)}), bf16[1,64,256]{2,1,0:T(8,128)(2,1)}) %reduce-scatter.17.cloned.1.call-update) | async-done | bytes 32784 | tf_op jit(solution)/shard_map/reduce_scatter | solution.py:164
  279.1 56.8 %reduce-scatter.15.cloned.1.call-done = bf16[1,64,256]{2,1,0:T(8,128)(2,1)} async-done(((bf16[1,64,4096]{2,1,0:T(8,128)(2,1)}), bf16[1,64,256]{2,1,0:T(8,128)(2,1)}) %reduce-scatter.15.cloned.1.call-update) | async-done | bytes 32784 | tf_op jit(solution)/shard_map/reduce_scatter | solution.py:161
  337.3 92.5 %reduce-scatter.19.cloned.1.call-done = f32[320,512]{1,0:T(8,128)} async-done(((f32[5120,512]{1,0:T(8,128)}), f32[320,512]{1,0:T(8,128)}) %reduce-scatter.19.cloned.1.call-update) | async-done | bytes 655376
  429.7 92.7 %reduce-scatter.21.cloned.1.call-done = f32[320,512]{1,0:T(8,128)} async-done(((f32[5120,512]{1,0:T(8,128)}), f32[320,512]{1,0:T(8,128)}) %reduce-scatter.21.cloned.1.call-update) | async-done | bytes 655376
  (185 shorter events, 74.5 us)
Async XLA Ops:
  8.0 8.1 %copy-start.22 = (s32[320]{0:T(512)S(1)}, s32[320]{0:T(512)}, u32[]{:S(2)}) copy-start(s32[320]{0:T(512)} %param.16) | copy-start | bytes 3844
  8.0 60.8 %copy-start.20 = (bf16[320,512]{1,0:T(8,128)(2,1)S(1)}, bf16[320,512]{1,0:T(8,128)(2,1)}, u32[]{:S(2)}) copy-start(bf16[320,512]{1,0:T(8,128)(2,1)} %param.17) | copy-start | bytes 983044
  8.0 60.8 %copy-start.23 = (s32[320]{0:T(512)S(1)}, s32[320]{0:T(512)}, u32[]{:S(2)}) copy-start(s32[320]{0:T(512)} %param.20) | copy-start | bytes 3844
  8.1 60.8 %reduce-scatter.11.cloned.1.call-start = ((), (), s32[]{:S(2)}) async-start(), calls=%async_computation.8 | async-start | bytes 2359296 | tf_op jit(solution)/shard_map/reduce_scatter | solution.py:63
  12.8 61.8 %copy-start.12 = (bf16[320,512]{1,0:T(8,128)(2,1)S(1)}, bf16[320,512]{1,0:T(8,128)(2,1)}, u32[]{:S(2)}) copy-start(bf16[320,512]{1,0:T(8,128)(2,1)} %param.23) | copy-start | bytes 983044
  12.8 69.0 %reduce-scatter.13.cloned.1.call-start = ((), (), s32[]{:S(2)}) async-start(), calls=%async_computation.9 | async-start | bytes 2359296 | tf_op jit(solution)/shard_map/reduce_scatter | solution.py:66
  13.6 71.8 %all-gather.5.cloned.1.call-start = ((), (), s32[]{:S(2)}) async-start(), calls=%async_computation.6 | async-start | bytes 5570560 | tf_op jit(solution)/shard_map/all_gather | solution.py:44
  14.2 117.0 %all-gather.7.cloned.1.call-start = ((), (), s32[]{:S(2)}) async-start(), calls=%async_computation.7 | async-start | bytes 5570560 | tf_op jit(solution)/shard_map/all_gather | solution.py:45
  14.8 144.1 %all-gather.11.cloned.1.call-start = ((), (), s32[]{:S(2)}) async-start(), calls=%async_computation.12 | async-start | bytes 2359296 | tf_op jit(solution)/shard_map/all_gather | solution.py:150
  70.0 15.3 %copy-start.18 = (bf16[320,512]{1,0:T(8,128)(2,1)S(1)}, bf16[320,512]{1,0:T(8,128)(2,1)}, u32[]{:S(2)}) copy-start(bf16[320,512]{1,0:T(8,128)(2,1)} %param.13) | copy-start | bytes 983044
  85.0 101.8 %all-gather.9.cloned.1.call-start = ((), (), s32[]{:S(2)}) async-start(), calls=%async_computation.10 | async-start | bytes 2359296 | tf_op jit(solution)/shard_map/all_gather | solution.py:149
  144.7 19.0 %copy-start.14 = (bf16[320,256]{1,0:T(8,128)(2,1)}, bf16[320,256]{1,0:T(8,128)(2,1)S(1)}, u32[]{:S(2)}) copy-start(bf16[320,256]{1,0:T(8,128)(2,1)S(1)} %fusion.63) | copy-start | bytes 491524
  145.2 23.1 %copy-start.15 = (bf16[320,256]{1,0:T(8,128)(2,1)}, bf16[320,256]{1,0:T(8,128)(2,1)S(1)}, u32[]{:S(2)}) copy-start(bf16[320,256]{1,0:T(8,128)(2,1)S(1)} %fusion.62) | copy-start | bytes 491524
  145.7 22.7 %copy-start.16 = (bf16[320,256]{1,0:T(8,128)(2,1)}, bf16[320,256]{1,0:T(8,128)(2,1)S(1)}, u32[]{:S(2)}) copy-start(bf16[320,256]{1,0:T(8,128)(2,1)S(1)} %fusion.61) | copy-start | bytes 491524
  146.8 113.8 %reduce-scatter.17.cloned.1.call-start = ((), (), s32[]{:S(2)}) async-start(), calls=%async_computation.13 | async-start | bytes 557056 | tf_op jit(solution)/shard_map/reduce_scatter | solution.py:164
  162.4 9.0 %slice-start.12 = ((s8[6553600]{0:T(1024)(128)(4,1)}), s8[2359296]{0:T(1024)(128)(4,1)S(1)}, s32[]{:S(2)}) async-start(s8[6553600]{0:T(1024)(128)(4,1)} %bitcast.79), calls=%async_computation.28 | async-start | bytes 4718592
  163.8 172.1 %reduce-scatter.15.cloned.1.call-start = ((), (), s32[]{:S(2)}) async-start(), calls=%async_computation.11 | async-start | bytes 557056 | tf_op jit(solution)/shard_map/reduce_scatter | solution.py:161
  168.3 8.8 %slice-start.6 = ((s8[6553600]{0:T(1024)(128)(4,1)}), s8[4194304]{0:T(1024)(128)(4,1)S(1)}, s32[]{:S(2)}) async-start(s8[6553600]{0:T(1024)(128)(4,1)} %bitcast.73), calls=%async_computation.22 | async-start | bytes 8388608
  168.3 8.8 %slice-start.16 = ((s8[5242880]{0:T(1024)(128)(4,1)}), s8[4194304]{0:T(1024)(128)(4,1)S(1)}, s32[]{:S(2)}) async-start(s8[5242880]{0:T(1024)(128)(4,1)} %bitcast.83), calls=%async_computation.32 | async-start | bytes 8388608
  183.0 10.9 %copy-start.7 = (bf16[320,5120]{1,0:T(8,128)(2,1)}, bf16[320,5120]{1,0:T(8,128)(2,1)S(1)}, u32[]{:S(2)}) copy-start(bf16[320,5120]{1,0:T(8,128)(2,1)S(1)} %fusion.15) | copy-start | bytes 9830404
  191.6 238.1 %reduce-scatter.19.cloned.1.call-start = ((), (), s32[]{:S(2)}) async-start(), calls=%async_computation.14 | async-start | bytes 11141120
  211.1 311.3 %reduce-scatter.21.cloned.1.call-start = ((), (), s32[]{:S(2)}) async-start(), calls=%async_computation.15 | async-start | bytes 11141120
  238.7 29.5 %copy-start.2 = (bf16[320,5120]{1,0:T(8,128)(2,1)S(1)}, bf16[320,5120]{1,0:T(8,128)(2,1)}, u32[]{:S(2)}) copy-start(bf16[320,5120]{1,0:T(8,128)(2,1)} %copy-done.1) | copy-start | bytes 9830404
  260.6 10.1 %copy-start.4 = (bf16[320,5120]{1,0:T(8,128)(2,1)S(1)}, bf16[320,5120]{1,0:T(8,128)(2,1)}, u32[]{:S(2)}) copy-start(bf16[320,5120]{1,0:T(8,128)(2,1)} %copy-done.3) | copy-start | bytes 9830404
  (31 other events, 127.5 us)
Sparse Core Ops, SparseCore 0:
  13.0 33.6 reduce-scatter.10
  49.0 32.7 reduce-scatter.12
Sparse Core Ops, SparseCore 1:
  16.2 57.0 all-gather.4
  75.3 55.8 all-gather.6
  133.3 25.5 all-gather.10
  161.2 25.5 all-gather.8
  190.5 70.0 reduce-scatter.16
  264.1 71.7 reduce-scatter.14
  339.7 89.9 reduce-scatter.18
  433.6 88.7 reduce-scatter.20
where the time goes:
time: 539 us; the launch traced here: 530 us
  waiting for transfers between devices  297 us (55%)
  matrix products  81.8 us (15%)
  blocking collectives  52.4 us (10%)
  other arithmetic  43.2 us (8%)
  local copies, waits for them, and re-layouts  36.8 us (7%)
  between operations  17.3 us (3%)
    unnamed x12, waiting for transfers between devices  187 us
    reduce_scatter x1, waiting for transfers between devices, shards(): lax.psum_scatter(image_key.astype(jnp.bfloat16), 'seq', scatter_dimension...  56.8 us
    unnamed x1, blocking collectives  52.4 us
    unnamed x95, local copies, waits for them, and re-layouts  32.4 us
    dot_general x16, matrix products, pair_scores(): jnp.einsum('id,jd->ij', left, right, preferred_element_type=jnp.float32)  28.7 us
    reduce_scatter x1, waiting for transfers between devices, shards(): lax.psum_scatter(image_value.astype(jnp.bfloat16), 'seq', scatter_dimensi...  21.8 us
    div x1, other arithmetic, shards(): probs = weights / row_total[:, None]  12.3 us
    all_gather x1, waiting for transfers between devices, shards(): lax.all_gather(slot_value_grad, 'vis', axis=2, tiled=True)  11.9 us
  transfers between devices with their start and end apart: 10, of which 8 were waited for; matrix products, arithmetic and copies ran while one was open for 28% of the time, Pallas kernels for 0%

commit v1 on v0

v1 whole, which is shorter than its diff:
```python
import functools
import math

import jax
import jax.numpy as jnp
from jax import lax
from jax.experimental import pallas as pl
from jax.experimental.pallas import tpu as pltpu
from jax.sharding import PartitionSpec as P

HD = 128
TD = 320
NX = 4
CH = TD * NX
NC = 3
TILE = 256
NQ = CH // TILE
NK = 2 * NQ + 1
LAT = 64
SLOTS = 4
IMAGES = 8
WD = 512
SCALE = 1.0 / math.sqrt(HD)
BIG = -1e30
MESH = pl.DeviceIdType.MESH
F32, BF16, I32 = jnp.float32, jnp.bfloat16, jnp.int32

NT = (((1,), (1,)), ((), ()))
NN = (((1,), (0,)), ((), ()))


def dot(a, b, dims=NN):
    return lax.dot_general(a, b, dims, preferred_element_type=F32)


def fold(a, op):
    return op(a.reshape(a.shape[0] // 8, 8, a.shape[1]), axis=0)


def kernel(
    docs_ref, tok_ref, img_ref, gate_ref, q_ref, k_ref, v_ref, cq_ref, do_ref, lk_ref, lv_ref,
    mixed_ref, qg_ref, kg_ref, vg_ref, cqg_ref, lkg_ref, lvg_ref,
    kbuf, vbuf, qbuf, dobuf, dol, kt, vt, sbuf, pbuf, maxes, dvec, starts, dqt,
    cown, cx, crow, cz,
    latk, latv, lks, lvs, gk, gv, cross, latsend, latrecv,
    obuf, dqb, part_k, part_v, own_k, own_v, got_k, got_v, sum_k, sum_v,
    o_in, dq_in, dk_in, dv_in,
    a_send, a_recv, z_send, z_recv, c_send, c_recv, l_send, l_recv, g_send, g_recv,
    p_send, p_recv, b_send, b_recv,
):
    s = lax.axis_index("seq")
    v = lax.axis_index("vis")
    x = lax.rem(s, NX)
    z = lax.div(s, NX)

    def xpeer(d):
        return lax.rem(x + d, NX)

    def remote(src, dst, ssem, rsem, seq, vis):
        return pltpu.make_async_remote_copy(
            src_ref=src, dst_ref=dst, send_sem=ssem, recv_sem=rsem,
            device_id=(seq, vis), device_id_type=MESH,
        )

    def rows(i, n=TD):
        return pl.ds(pl.multiple_of(i * n, n), n)

    def cols(i, n=HD):
        return pl.ds(pl.multiple_of(i * n, n), n)

    barrier = pltpu.get_barrier_semaphore()

    def greet(seq, vis):
        pl.semaphore_signal(barrier, inc=1, device_id=(seq, vis), device_id_type=MESH)

    for d in range(1, NX):
        greet(z * NX + xpeer(d), v)
        greet(lax.rem(z + d, NX) * NX + x, v)
    for d in range(1, IMAGES):
        greet(s, lax.rem(v + d, IMAGES))
    half = lax.rem(s, 2)
    head_group = lax.div(s, 2)
    own_piece = head_group == v
    for i in range(16):
        @pl.when(jnp.logical_not(jnp.logical_and(s == i, own_piece)))
        def _():
            greet(jnp.int32(i), head_group)
    pl.semaphore_wait(barrier, 13 + 16 - jnp.where(own_piece, 1, 0))

    docs = docs_ref[...]
    row_id = lax.broadcasted_iota(I32, (8, HD), 0)
    counts = jnp.zeros((8, HD), F32)
    for d in range(1, 4):
        c = jnp.sum(jnp.where(docs < d, 1.0, 0.0), axis=1, keepdims=True)
        counts = jnp.where(row_id == d, c, counts)
    cown[...] = counts

    ins = (k_ref, v_ref, q_ref, do_ref)
    bufs = (kbuf, vbuf, qbuf, dobuf)
    base = (2 * CH, 2 * CH, 0, 0)

    def a_copy(arr, d):
        p = xpeer(d)
        return remote(
            ins[arr].at[:, cols(p)],
            bufs[arr].at[pl.ds(pl.multiple_of(base[arr] + x * TD, TD), TD), :],
            a_send.at[arr, d - 1], a_recv.at[arr, d - 1], z * NX + p, v,
        )

    def a_wait(arr, d):
        p = lax.rem(x + NX - d, NX)
        here = bufs[arr].at[pl.ds(pl.multiple_of(base[arr] + p * TD, TD), TD), :]
        remote(here, here, a_send.at[arr, d - 1], a_recv.at[arr, d - 1], s, v).wait_recv()

    def c_copy(stage, d):
        if stage == 0:
            return remote(cown, cx.at[d - 1], c_send.at[0, d - 1], c_recv.at[0, d - 1],
                          z * NX + xpeer(d), v)
        return remote(crow, cz.at[d - 1], c_send.at[1, d - 1], c_recv.at[1, d - 1],
                      lax.rem(z + d, NX) * NX + x, v)

    def z_copy(arr, dz, d):
        p = lax.rem(x + NX - d, NX)
        src = bufs[arr].at[pl.ds(pl.multiple_of(2 * CH + p * TD, TD), TD), :]
        dst = bufs[arr].at[pl.ds(pl.multiple_of((2 - dz) * CH + p * TD, TD), TD), :]
        return remote(src, dst, z_send.at[arr, dz - 1, d], z_recv.at[arr, dz - 1, d], s + dz * NX, v)

    def z_start(arr, d):
        for dz in (1, 2):
            @pl.when(z + dz < NX)
            def _():
                z_copy(arr, dz, d).start()

    def z_wait(arr, dz):
        for d in range(NX):
            p = lax.rem(x + NX - d, NX)
            here = bufs[arr].at[pl.ds(pl.multiple_of((2 - dz) * CH + p * TD, TD), TD), :]
            remote(here, here, z_send.at[arr, dz - 1, d], z_recv.at[arr, dz - 1, d], s, v).wait_recv()

    for arr in (0, 1):
        for d in (1, 3, 2):
            a_copy(arr, d).start()
    for d in (1, 3, 2):
        c_copy(0, d).start()
    for arr in range(4):
        bufs[arr][pl.ds(pl.multiple_of(base[arr] + x * TD, TD), TD), :] = ins[arr][:, cols(x)]
    for arr in (0, 1):
        z_start(arr, 0)
    for arr in (2, 3):
        for d in (1, 3, 2):
            a_copy(arr, d).start()

    lins, lbufs = (lk_ref, lv_ref), (latk, latv)

    def l_copy(arr, d):
        p = lax.rem(v + d, IMAGES)
        return remote(lins[arr].at[0, :, cols(p, WD)], lbufs[arr].at[v],
                      l_send.at[arr, d - 1], l_recv.at[arr, d - 1], s, p)

    for arr in (0, 1):
        for d in range(1, IMAGES):
            l_copy(arr, d).start()
        lbufs[arr][v] = lins[arr][0, :, cols(v, WD)]

    for arr in (0, 1):
        for d in (1, 3, 2):
            a_wait(arr, d)
            z_start(arr, d)

    for d in range(1, NX):
        here = cx.at[d - 1]
        remote(here, here, c_send.at[0, d - 1], c_recv.at[0, d - 1], s, v).wait_recv()
    crow[...] = cown[...] + cx[0] + cx[1] + cx[2]
    for d in range(1, NX):
        c_copy(1, d).start()
    for d in (1, 3, 2):
        a_wait(2, d)
    for d in range(1, NX):
        here = cz.at[d - 1]
        remote(here, here, c_send.at[1, d - 1], c_recv.at[1, d - 1], s, v).wait_recv()
    before = crow[...] + cz[0] + cz[1] + cz[2]
    pos = lax.broadcasted_iota(I32, (8, CH), 1)
    start = jnp.zeros((8, CH), I32)
    for d in range(1, 4):
        b = before[d:d + 1, 0:1].astype(I32)
        start = jnp.where(b <= pos + z * CH, b, start)
    starts[...] = start - (z - 2) * CH

    maxes[...] = jnp.full_like(maxes, BIG)
    key_iota = lax.broadcasted_iota(I32, (TILE, TILE), 0)
    query_iota = lax.broadcasted_iota(I32, (TILE, TILE), 1)

    def tile(i):
        return pl.ds(pl.multiple_of(i * TILE, TILE), TILE)

    def score_chunk(slot):
        def per_query(t, _):
            first = starts[0:1, tile(t)]
            qt = qbuf[tile(t), :]

            def per_key(c, _):
                raw = dot(kbuf[tile(c), :], qt, NT)
                kpos = key_iota + c * TILE
                kept = (kpos >= first) & (kpos <= query_iota + (2 * CH + t * TILE))
                raw = jnp.where(kept, raw, BIG)
                sbuf[t, tile(c - t), :] = raw
                maxes[:, tile(t)] = jnp.maximum(maxes[:, tile(t)], fold(raw, jnp.max))
                return 0

            lo = jnp.maximum(t, slot * NQ)
            hi = jnp.minimum(t + NK, (slot + 1) * NQ)
            return lax.fori_loop(lo, hi, per_key, 0)

        lax.fori_loop(0, NQ, per_query, 0)

    def flip(src, dst, slot):
        def step(c, _):
            dst[:, tile(c)] = src[tile(c), :].astype(F32).T.astype(BF16)
            return 0

        lax.fori_loop(slot * NQ, (slot + 1) * NQ, step, 0)

    score_chunk(2)
    flip(kbuf, kt, 2)
    flip(vbuf, vt, 2)

    for arr in (0, 1):
        for d in range(1, IMAGES):
            here = lbufs[arr].at[lax.rem(v + IMAGES - d, IMAGES)]
            remote(here, here, l_send.at[arr, d - 1], l_recv.at[arr, d - 1], s, v).wait_recv()
    for i in range(SLOTS):
        lks[i * LAT:(i + 1) * LAT, :] = latk[img_ref[i]]
        lvs[i * LAT:(i + 1) * LAT, :] = latv[img_ref[i]]
    slot_of = lax.broadcasted_iota(I32, (SLOTS * LAT, TD), 0) // LAT
    seen = slot_of == tok_ref[...]
    any_image = tok_ref[...] < SLOTS
    gate = jnp.tanh(gate_ref[...])
    for h in range(NX):
        sl = slice(h * HD, (h + 1) * HD)
        lkh, lvh, cqh = lks[:, sl], lvs[:, sl], cq_ref[:, sl]
        raw = dot(lkh, cqh, NT)
        raw = jnp.where(seen, raw * SCALE, BIG)
        w = jnp.where(seen, jnp.exp(raw - jnp.max(raw, axis=0, keepdims=True)), 0.0)
        total = jnp.where(any_image, jnp.sum(w, axis=0, keepdims=True), 1.0)
        probs = w / total
        low = probs.astype(BF16)
        out = dot(lvh.astype(F32).T.astype(BF16), low).T
        cross[:, sl] = gate[:, sl] * out
        back = (gate[:, sl] * do_ref[:, sl].astype(F32)).astype(BF16)
        gp = dot(lvh, back, NT)
        cdot = jnp.sum(probs * gp, axis=0, keepdims=True)
        ds = (probs * (gp - cdot) * SCALE).astype(BF16)
        cqg_ref[:, sl] = dot(lkh.astype(F32).T.astype(BF16), ds).T
        gk[:, sl] = dot(ds, cqh).astype(BF16).astype(F32)
        gv[:, sl] = dot(low, back).astype(BF16).astype(F32)

    for m in range(IMAGES):
        for n, g in enumerate((gk, gv)):
            acc = jnp.zeros((LAT, WD), F32)
            for i in range(SLOTS):
                acc = acc + jnp.where(img_ref[i] == m, 1.0, 0.0) * g[i * LAT:(i + 1) * LAT, :]
            acc = acc.astype(BF16)
            latsend[m, 0, n] = acc[:, 0:256]
            latsend[m, 1, n] = acc[:, 256:512]

    def g_copy(m, h):
        return remote(latsend.at[m, h], latrecv.at[s], g_send.at[m, h], g_recv.at[s], 2 * v + h,
                      jnp.int32(m))

    def g_mine(m, h):
        return jnp.logical_and(s == 2 * v + h, v == m)

    for m in range(IMAGES):
        for h in range(2):
            @pl.when(jnp.logical_not(g_mine(m, h)))
            def _():
                g_copy(m, h).start()

    @pl.when(own_piece)
    def _():
        latrecv[s] = latsend[v, half]

    @pl.when(z >= 1)
    def _():
        z_wait(0, 1)
        score_chunk(1)
        flip(kbuf, kt, 1)

    @pl.when(z >= 2)
    def _():
        z_wait(0, 2)
        score_chunk(0)
        flip(kbuf, kt, 0)

    @pl.when(z >= 1)
    def _():
        z_wait(1, 1)
        flip(vbuf, vt, 1)

    @pl.when(z >= 2)
    def _():
        z_wait(1, 2)
        flip(vbuf, vt, 0)

    for d in (1, 3, 2):
        a_wait(3, d)

    low_tile = (2 - jnp.minimum(z, 2)) * NQ

    def forward(t, _):
        top = jnp.max(maxes[:, tile(t)], axis=0, keepdims=True)

        def per_key(c, carry):
            total, out = carry
            p = jnp.exp((sbuf[t, tile(c - t), :] - top) * SCALE)
            pb = p.astype(BF16)
            pbuf[t, tile(c - t), :] = pb
            return total + fold(p, jnp.sum), out + dot(vt[:, tile(c)], pb)

        total, out = lax.fori_loop(
            jnp.maximum(t, low_tile), t + NK, per_key,
            (jnp.zeros((8, TILE), F32), jnp.zeros((HD, TILE), F32)),
        )
        inv = 1.0 / jnp.sum(total, axis=0, keepdims=True)
        out = out * inv
        obuf[tile(t), :] = out.T.astype(BF16)
        dot_ = dobuf[tile(t), :].astype(F32).T
        dvec[:, tile(t)] = jnp.broadcast_to(jnp.sum(dot_ * out, axis=0, keepdims=True) * inv, (8, TILE))
        dol[tile(t), :] = (dot_ * inv).T.astype(BF16)
        dqt[t] = jnp.zeros((HD, TILE), F32)
        return 0

    lax.fori_loop(0, NQ, forward, 0)

    outs = (obuf, dqb, sum_k, sum_v)
    backs = (o_in, dq_in, dk_in, dv_in)

    def b_copy(arr, d):
        p = xpeer(d)
        return remote(outs[arr].at[rows(p), :], backs[arr].at[:, cols(x)],
                      b_send.at[arr, d - 1], b_recv.at[arr, d - 1], z * NX + p, v)

    def b_wait(arr, d):
        p = lax.rem(x + NX - d, NX)
        here = backs[arr].at[:, cols(p)]
        remote(here, here, b_send.at[arr, d - 1], b_recv.at[arr, d - 1], s, v).wait_recv()

    def b_own(arr):
        backs[arr][:, cols(x)] = outs[arr][rows(x), :]

    for d in (1, 3, 2):
        b_copy(0, d).start()
    b_own(0)

    def backward(slot):
        def per_key(c, _):
            kc, vc, ktc = kbuf[tile(c), :], vbuf[tile(c), :], kt[:, tile(c)]

            def per_query(t, carry):
                dk, dv = carry
                pb = pbuf[t, tile(c - t), :]
                dolt = dol[tile(t), :]
                dp = dot(vc, dolt, NT)
                ds = (pb.astype(F32) * (dp - dvec[0:1, tile(t)])).astype(BF16)
                dqt[t] += dot(ktc, ds)
                return dk + dot(ds, qbuf[tile(t), :]), dv + dot(pb, dolt)

            zero = jnp.zeros((TILE, HD), F32)
            dk, dv = lax.fori_loop(
                jnp.maximum(0, c - 2 * NQ), jnp.minimum(NQ - 1, c) + 1, per_query, (zero, zero))
            dk = dk * SCALE
            if slot == 2:
                own_k[tile(c - 2 * NQ), :] = dk
                own_v[tile(c - 2 * NQ), :] = dv
            else:
                part_k[tile(c), :] = dk.astype(BF16)
                part_v[tile(c), :] = dv.astype(BF16)
            return 0

        lax.fori_loop(slot * NQ, (slot + 1) * NQ, per_key, 0)

    parts, gots = (part_k, part_v), (got_k, got_v)

    def p_copy(arr, dz, p):
        return remote(parts[arr].at[pl.ds((2 - dz) * CH + p * TD, TD), :],
                      gots[arr].at[pl.ds((dz - 1) * CH + p * TD, TD), :],
                      p_send.at[arr, dz - 1, p], p_recv.at[arr, dz - 1, p], s - dz * NX, v)

    for dz in (2, 1):
        @pl.when(z >= dz)
        def _():
            backward(2 - dz)
            for p in range(NX):
                for arr in (0, 1):
                    p_copy(arr, dz, p).start()

    backward(2)
    for t in range(NQ):
        dqb[t * TILE:(t + 1) * TILE, :] = (dqt[t] * SCALE).T.astype(BF16)
    for d in (1, 3, 2):
        b_copy(1, d).start()
    b_own(1)

    for d in (1, 3, 2):
        b_wait(0, d)
    mixed_ref[...] = (o_in[...].astype(F32) + cross[...]).astype(BF16)
    for i in range(16):
        @pl.when(jnp.logical_not(jnp.logical_and(s == i, own_piece)))
        def _():
            here = latrecv.at[i]
            remote(here, here, g_send.at[0, 0], g_recv.at[i], s, v).wait_recv()
    for n, g in enumerate((lkg_ref, lvg_ref)):
        acc = latrecv[0, n].astype(F32)
        for i in range(1, 16):
            acc = acc + latrecv[i, n].astype(F32)
        g[0] = acc

    for p in range(NX):
        sl = slice(p * TD, (p + 1) * TD)
        for arr, (own, out) in enumerate(((own_k, sum_k), (own_v, sum_v))):
            for dz in (1, 2):
                @pl.when(z + dz < NX)
                def _():
                    here = gots[arr].at[pl.ds((dz - 1) * CH + p * TD, TD), :]
                    remote(here, here, p_send.at[arr, dz - 1, p], p_recv.at[arr, dz - 1, p], s, v).wait_recv()
                    own[sl, :] += here[...].astype(F32)
            out[sl, :] = own[sl, :].astype(BF16)
    for arr in (2, 3):
        for d in (1, 3, 2):
            b_copy(arr, d).start()
        b_own(arr)
    for arr, out in ((1, qg_ref), (2, kg_ref), (3, vg_ref)):
        for d in (1, 3, 2):
            b_wait(arr, d)
        out[...] = backs[arr][...].astype(F32)

    for d in range(1, NX):
        for arr in range(4):
            a_copy(arr, d).wait_send()
            b_copy(arr, d).wait_send()
        for stage in range(2):
            c_copy(stage, d).wait_send()
    for arr in (0, 1):
        for d in range(1, IMAGES):
            l_copy(arr, d).wait_send()
        for dz in (1, 2):
            @pl.when(z + dz < NX)
            def _():
                for d in range(NX):
                    z_copy(arr, dz, d).wait_send()

            @pl.when(z >= dz)
            def _():
                for p in range(NX):
                    p_copy(arr, dz, p).wait_send()
    for m in range(IMAGES):
        for h in range(2):
            @pl.when(jnp.logical_not(g_mine(m, h)))
            def _():
                g_copy(m, h).wait_send()


def shards(query, key, value, doc_ids, cross_query, latent_key, latent_value, token_slot,
           slot_image, cross_gate, out_grad):
    vm = pl.BlockSpec(memory_space=pltpu.VMEM)
    sm = pl.BlockSpec(memory_space=pltpu.SMEM)
    dma = pltpu.SemaphoreType.DMA
    scratch = [
        pltpu.VMEM((NC * CH, HD), BF16), pltpu.VMEM((NC * CH, HD), BF16),
        pltpu.VMEM((CH, HD), BF16), pltpu.VMEM((CH, HD), BF16), pltpu.VMEM((CH, HD), BF16),
        pltpu.VMEM((HD, NC * CH), BF16), pltpu.VMEM((HD, NC * CH), BF16),
        pltpu.VMEM((NQ, NK * TILE, TILE), F32), pltpu.VMEM((NQ, NK * TILE, TILE), BF16),
        pltpu.VMEM((8, CH), F32), pltpu.VMEM((8, CH), F32), pltpu.VMEM((8, CH), I32),
        pltpu.VMEM((NQ, HD, TILE), F32),
        pltpu.VMEM((8, HD), F32), pltpu.VMEM((3, 8, HD), F32),
        pltpu.VMEM((8, HD), F32), pltpu.VMEM((3, 8, HD), F32),
        pltpu.VMEM((IMAGES, LAT, WD), BF16), pltpu.VMEM((IMAGES, LAT, WD), BF16),
        pltpu.VMEM((SLOTS * LAT, WD), BF16), pltpu.VMEM((SLOTS * LAT, WD), BF16),
        pltpu.VMEM((SLOTS * LAT, WD), F32), pltpu.VMEM((SLOTS * LAT, WD), F32),
        pltpu.VMEM((TD, WD), F32),
        pltpu.VMEM((IMAGES, 2, 2, LAT, 256), BF16), pltpu.VMEM((16, 2, LAT, 256), BF16),
        pltpu.VMEM((CH, HD), BF16), pltpu.VMEM((CH, HD), BF16),
        pltpu.VMEM((2 * CH, HD), BF16), pltpu.VMEM((2 * CH, HD), BF16),
        pltpu.VMEM((CH, HD), F32), pltpu.VMEM((CH, HD), F32),
        pltpu.VMEM((2 * CH, HD), BF16), pltpu.VMEM((2 * CH, HD), BF16),
        pltpu.VMEM((CH, HD), BF16), pltpu.VMEM((CH, HD), BF16),
        pltpu.VMEM((TD, WD), BF16), pltpu.VMEM((TD, WD), BF16),
        pltpu.VMEM((TD, WD), BF16), pltpu.VMEM((TD, WD), BF16),
        dma((4, 3)), dma((4, 3)),
        dma((2, 2, 4)), dma((2, 2, 4)),
        dma((2, 3)), dma((2, 3)),
        dma((2, 7)), dma((2, 7)),
        dma((8, 2)), dma((16,)),
        dma((2, 2, 4)), dma((2, 2, 4)),
        dma((4, 3)), dma((4, 3)),
    ]
    full = jax.ShapeDtypeStruct((TD, WD), F32)
    lat = jax.ShapeDtypeStruct((1, LAT, 256), F32)
    return pl.pallas_call(
        kernel,
        out_shape=(jax.ShapeDtypeStruct((TD, WD), BF16), full, full, full, full, lat, lat),
        in_specs=[vm, vm, sm] + [vm] * 8,
        out_specs=(vm,) * 7,
        scratch_shapes=scratch,
        cost_estimate=pl.CostEstimate(flops=6_500_000_000, bytes_accessed=8_000_000, transcendentals=4_000_000),
        compiler_params=pltpu.CompilerParams(
            collective_id=0, has_side_effects=True, vmem_limit_bytes=58 * 1024 * 1024),
    )(
        doc_ids.reshape(1, TD), token_slot.reshape(1, TD), slot_image, cross_gate.reshape(1, WD),
        query, key, value, cross_query, out_grad, latent_key, latent_value,
    )


def solution(mesh):
    own = P("seq", "vis")
    lat_in = P("vis", None, None)
    lat_out = P("vis", None, "seq")
    return jax.shard_map(
        shards,
        mesh=mesh,
        in_specs=(own, own, own, P("seq"), own, lat_in, lat_in, P("seq"), P("seq"), P("vis"), own),
        out_specs=(own, own, own, own, own, lat_out, lat_out),
        check_vma=False,
    )
```

time: 539 us -> 137 us (0.25)
  the two profiles are of different devices: /device:TPU:59 before, /device:TPU:48 now
where the time goes in v1:
time: 137 us
  Pallas kernels  126 us (92%)
  local copies, waits for them, and re-layouts  9.93 us (7%)
    pallas_call x1, Pallas kernels, shards(): pl.pallas_call(kernel, out_shape=(jax.ShapeDtypeStruct((TD, WD), BF16), f...  126 us
    unnamed x21, local copies, waits for them, and re-layouts  8.11 us

profile of v1, /device:TPU:48, one launch (start us, length us, event | category | flops | bytes accessed | tf_op | source)
XLA Modules:
  0.0 136.9 jit_solution(4865739230568405299)
XLA Ops:
  0.6 0.0 copy-start.6
  0.6 1.3 reshape.23.docs_ref
  1.9 0.0 copy-done.6
  1.9 0.6 reshape.24.tok_ref
  2.5 126.3 %shard_map.162 = (bf16[320,512]{1,0:T(8,128)(2,1)}, f32[320,512]{1,0:T(8,128)}, f32[320,512]{1,0:T(8,128)}, f32[320,512]{1,0:T(8,128)}, f32[320,512]{1,0:T(8,128...) custom-call(s32[1,320]{1,0:T(1,128)} %reshape.23.docs_ref, s32[1,320]{1,0:T(1,128)} %reshape.24.tok_ref, s32[4]{0:T(128)} %img_ref.1, ...), custom_call_target="tpu_custom_call" | custom-call | flops 6499999744 | bytes 8000000 | tf_op jit(solution)/shard_map/pallas_call | solution.py:499
  128.8 0.0 copy-start.3
  128.8 1.8 %copy.25 = bf16[320,512]{1,0:T(8,128)(2,1)} copy(bf16[320,512]{1,0:T(8,128)(2,1)} %get-tuple-element.14) | data formatting | bytes 655360
  130.6 0.0 copy-done.3
  130.6 0.0 copy-start.2
  130.6 0.8 copy.26
  131.4 0.5 copy-done.2
  131.9 0.0 copy-start.1
  131.9 0.8 copy.27
  132.8 0.5 copy-done.1
  133.3 0.0 copy-start
  133.3 0.8 copy.28
  134.1 0.5 copy-done
  134.6 0.0 copy-start.5
  134.6 0.8 copy.29
  135.4 0.0 copy-done.5
  135.4 0.0 copy-start.4
  135.4 0.6 copy.30
  136.1 0.2 copy-done.4
  136.3 0.6 copy.31
Async XLA Ops:
  0.6 1.3 copy-start.6
  128.8 1.8 %copy-start.3 = (f32[320,512]{1,0:T(8,128)S(1)}, f32[320,512]{1,0:T(8,128)}, u32[]{:S(2)}) copy-start(f32[320,512]{1,0:T(8,128)} %get-tuple-element.15) | copy-start | bytes 1966084
  130.6 1.3 copy-start.2
  131.9 1.3 copy-start.1
  133.3 1.3 copy-start
  134.6 0.9 copy-start.5
  135.4 0.9 copy-start.4

commit v2 on v1

v2 whole, which is shorter than its diff:
```python
import functools
import math

import jax
import jax.numpy as jnp
from jax import lax
from jax.experimental import pallas as pl
from jax.experimental.pallas import tpu as pltpu
from jax.sharding import PartitionSpec as P

HD = 128
TD = 320
NX = 4
CH = TD * NX
NC = 3
TILE = 256
NQ = CH // TILE
LAT = 64
SLOTS = 4
IMAGES = 8
WD = 512
SCALE = 1.0 / math.sqrt(HD)
BIG = -1e30
MESH = pl.DeviceIdType.MESH
F32, BF16, I32 = jnp.float32, jnp.bfloat16, jnp.int32

NT = (((1,), (1,)), ((), ()))
NN = (((1,), (0,)), ((), ()))


def dot(a, b, dims=NN):
    return lax.dot_general(a, b, dims, preferred_element_type=F32)


def fold(a, op):
    return op(a.reshape(a.shape[0] // 8, 8, a.shape[1]), axis=0)

LOG2E = 1.4426950408889634

FWD_TILES = (
    tuple((c * TILE, TILE, 0, (c + 1) * TILE) for c in range(NQ)),
    tuple((c * TILE, TILE, 0, CH) for c in range(NQ)),
    tuple((c * TILE, TILE, c * TILE, CH - c * TILE) for c in range(NQ)),
)
BWD_TILES = (FWD_TILES[0], ((0, CH // 2, 0, CH), (CH // 2, CH // 2, 0, CH)), FWD_TILES[2])
ORDER = (0, 1, 3, 2)


def kernel(
    docs_ref, tok_ref, img_ref, gate_ref, q_ref, k_ref, v_ref, cq_ref, do_ref, lk_ref, lv_ref,
    mixed_ref, qg_ref, kg_ref, vg_ref, cqg_ref, lkg_ref, lvg_ref,
    kbuf, vbuf, qbuf, dobuf, dol, kt, vt, sbuf, pbuf, opart, maxes, sums, starts, dot_t, dqt,
    cown, cx, crow, cz, cqv, dov, stage,
    latk, latv, lks, lvs, gk, gv, cross, latsend, latx, latz, latzin, latp, latin,
    obuf, dqb, part_k, part_v, own_k, own_v, got_k, got_v, sum_k, sum_v,
    o_in, dq_in, dk_in, dv_in,
    a_send, a_recv, z_send, z_recv, c_send, c_recv, l_send, l_recv, gx_send, gx_recv, gz_send, gz_recv,
    gp_send, gp_recv, p_send, p_recv, b_send, b_recv, f_send, f_recv, own_sem,
):
    s = lax.axis_index("seq")
    v = lax.axis_index("vis")
    x = lax.rem(s, NX)
    z = lax.div(s, NX)

    def xpeer(d):
        return lax.rem(x + d, NX)

    def zpeer(d):
        return lax.rem(z + d, NX)

    def remote(src, dst, ssem, rsem, seq, vis):
        return pltpu.make_async_remote_copy(
            src_ref=src, dst_ref=dst, send_sem=ssem, recv_sem=rsem,
            device_id=(seq, vis), device_id_type=MESH,
        )

    def landed(here, rsem):
        remote(here, here, rsem, rsem, s, v).wait_recv()

    def rows(i, n=TD):
        return pl.ds(pl.multiple_of(i * n, n), n)

    def cols(i, n=HD):
        return pl.ds(pl.multiple_of(i * n, n), n)

    def piece(slot, p):
        return pl.ds(pl.multiple_of(slot * CH + p * TD, TD), TD)

    barrier = pltpu.get_barrier_semaphore()

    def greet(seq, vis):
        pl.semaphore_signal(barrier, inc=1, device_id=(seq, vis), device_id_type=MESH)

    to_seq = 2 * v + lax.rem(z, 2)
    to_vis = 2 * x + lax.div(z, 2)
    from_seq = (2 * lax.rem(v, 2) + lax.rem(s, 2)) * NX + lax.div(v, 2)
    from_vis = lax.div(s, 2)
    stays = jnp.logical_and(to_seq == s, to_vis == v)
    moves = jnp.logical_not(stays)

    for d in range(1, NX):
        greet(z * NX + xpeer(d), v)
        greet(zpeer(d) * NX + x, v)
    for d in range(1, IMAGES):
        greet(s, lax.rem(v + d, IMAGES))

    @pl.when(moves)
    def _():
        greet(from_seq, from_vis)

    def own_copy(i):
        src, dst = (
            (k_ref.at[:, cols(x)], kbuf.at[piece(2, x), :]),
            (v_ref.at[:, cols(x)], vbuf.at[piece(2, x), :]),
            (q_ref.at[:, cols(x)], qbuf.at[piece(0, x), :]),
            (do_ref.at[:, cols(x)], dobuf.at[piece(0, x), :]),
            (lk_ref.at[0, :, cols(v, WD)], latk.at[v]),
            (lv_ref.at[0, :, cols(v, WD)], latv.at[v]),
            (cq_ref, cqv),
            (do_ref, dov),
        )[i]
        return pltpu.make_async_copy(src, dst, own_sem.at[i])

    for i in range(8):
        own_copy(i).start()

    docs = docs_ref[...]
    row_id = lax.broadcasted_iota(I32, (8, HD), 0)
    counts = jnp.zeros((8, HD), F32)
    for d in range(1, 4):
        c = jnp.sum(jnp.where(docs < d, 1.0, 0.0), axis=1, keepdims=True)
        counts = jnp.where(row_id == d, c, counts)
    cown[...] = counts
    pl.semaphore_wait(barrier, 13 + jnp.where(stays, 0, 1))

    ins = (k_ref, v_ref, q_ref, do_ref)
    bufs = (kbuf, vbuf, qbuf, dobuf)
    base = (2, 2, 0, 0)

    def a_copy(arr, d):
        p = xpeer(d)
        return remote(ins[arr].at[:, cols(p)], bufs[arr].at[piece(base[arr], x), :],
                      a_send.at[arr, d - 1], a_recv.at[arr, d - 1], z * NX + p, v)

    def a_wait(arr, d):
        landed(bufs[arr].at[piece(base[arr], xpeer(NX - d)), :], a_recv.at[arr, d - 1])

    def c_copy(step, d):
        if step == 0:
            return remote(cown, cx.at[d - 1], c_send.at[0, d - 1], c_recv.at[0, d - 1],
                          z * NX + xpeer(d), v)
        return remote(crow, cz.at[d - 1], c_send.at[1, d - 1], c_recv.at[1, d - 1],
                      zpeer(d) * NX + x, v)

    def z_copy(arr, dz, i):
        p = xpeer(NX - ORDER[i])
        src = ins[arr].at[:, cols(x)] if i == 0 else bufs[arr].at[piece(2, p), :]
        return remote(src, bufs[arr].at[piece(2 - dz, p), :],
                      z_send.at[arr, dz - 1, i], z_recv.at[arr, dz - 1, i], s + dz * NX, v)

    def f_copy(arr, i):
        p = xpeer(NX - ORDER[i])
        src = ins[arr].at[:, cols(x)] if i == 0 else bufs[arr].at[piece(2, p), :]
        return remote(src, stage.at[arr, i], z_send.at[arr, 1, i], f_recv.at[arr, i], s + 3 * NX, v)

    def f_on(arr, i):
        p = xpeer(NX - ORDER[i])
        return remote(stage.at[arr, i], bufs[arr].at[piece(0, p), :],
                      f_send.at[arr, i], z_recv.at[arr, 1, i], s - NX, v)

    def z_start(arr, i):
        if i < 2:
            @pl.when(z == 0)
            def _():
                f_copy(arr, i).start()

            @pl.when(z == 1)
            def _():
                z_copy(arr, 2, i).start()
        else:
            @pl.when(z <= 1)
            def _():
                z_copy(arr, 2, i).start()

        @pl.when(z <= 2)
        def _():
            z_copy(arr, 1, i).start()

    def f_relay(arr):
        @pl.when(z == 3)
        def _():
            for i in range(2):
                landed(stage.at[arr, i], f_recv.at[arr, i])
                f_on(arr, i).start()

    def z_wait(arr, dz):
        for i in range(NX):
            landed(bufs[arr].at[piece(2 - dz, xpeer(NX - ORDER[i])), :], z_recv.at[arr, dz - 1, i])

    for arr in (0, 1):
        z_start(arr, 0)
        for d in ORDER[1:]:
            a_copy(arr, d).start()
    for d in ORDER[1:]:
        c_copy(0, d).start()
    for arr in (2, 3):
        for d in ORDER[1:]:
            a_copy(arr, d).start()

    lins, lbufs = (lk_ref, lv_ref), (latk, latv)

    def l_copy(arr, d):
        p = lax.rem(v + d, IMAGES)
        return remote(lins[arr].at[0, :, cols(p, WD)], lbufs[arr].at[v],
                      l_send.at[arr, d - 1], l_recv.at[arr, d - 1], s, p)

    for arr in (0, 1):
        for d in range(1, IMAGES):
            l_copy(arr, d).start()

    for arr in (0, 1):
        for i in range(1, NX):
            a_wait(arr, ORDER[i])
            z_start(arr, i)
    f_relay(0)

    for d in ORDER[1:]:
        landed(cx.at[d - 1], c_recv.at[0, d - 1])
    crow[...] = cown[...] + cx[0] + cx[1] + cx[2]
    for d in range(1, NX):
        c_copy(1, d).start()
    for i in range(8):
        own_copy(i).wait()
    for d in ORDER[1:]:
        a_wait(2, d)
    f_relay(1)
    for d in range(1, NX):
        landed(cz.at[d - 1], c_recv.at[1, d - 1])
    before = crow[...] + cz[0] + cz[1] + cz[2]
    pos = lax.broadcasted_iota(I32, (8, CH), 1)
    start = jnp.zeros((8, CH), I32)
    for d in range(1, 4):
        b = before[d:d + 1, 0:1].astype(I32)
        start = jnp.where(b <= pos + z * CH, b, start)
    starts[...] = start - (z - 2) * CH

    for slot in range(NC):
        maxes[slot] = jnp.full((8, CH), BIG, F32)
        sums[slot] = jnp.zeros((8, CH), F32)
        opart[slot] = jnp.zeros((HD, CH), F32)

    def forward(slot):
        at = slot * CH
        kt[:, at:at + CH] = kbuf[at:at + CH, :].T
        vt[:, at:at + CH] = vbuf[at:at + CH, :].T
        for k0, kn, q0, qn in FWD_TILES[slot]:
            across = slice(q0, q0 + qn)
            raw = dot(kbuf[at + k0:at + k0 + kn, :], qbuf[across, :], NT)
            kpos = lax.broadcasted_iota(I32, (kn, qn), 0) + (at + k0)
            kept = kpos >= starts[0:1, across]
            if slot == 2:
                kept = kept & (kpos <= lax.broadcasted_iota(I32, (kn, qn), 1) + (at + q0))
            raw = jnp.where(kept, raw, BIG)
            sbuf[k0:k0 + kn, across] = raw
            maxes[slot, :, across] = jnp.maximum(maxes[slot, :, across], fold(raw, jnp.max))
        top = jnp.max(maxes[slot], axis=0, keepdims=True)
        maxes[slot] = jnp.broadcast_to(top, (8, CH))
        for k0, kn, q0, qn in FWD_TILES[slot]:
            across = slice(q0, q0 + qn)
            p = jnp.exp2((sbuf[k0:k0 + kn, across] - top[:, across]) * (SCALE * LOG2E))
            pb = p.astype(BF16)
            pbuf[at + k0:at + k0 + kn, across] = pb
            sums[slot, :, across] += fold(p, jnp.sum)
            opart[slot, :, across] += dot(vt[:, at + k0:at + k0 + kn], pb)

    forward(2)

    for arr in (0, 1):
        for d in range(1, IMAGES):
            landed(lbufs[arr].at[lax.rem(v + IMAGES - d, IMAGES)], l_recv.at[arr, d - 1])
    for i in range(SLOTS):
        lks[i * LAT:(i + 1) * LAT, :] = latk[img_ref[i]]
        lvs[i * LAT:(i + 1) * LAT, :] = latv[img_ref[i]]
    slot_of = lax.broadcasted_iota(I32, (SLOTS * LAT, TD), 0) // LAT
    seen = slot_of == tok_ref[...]
    any_image = tok_ref[...] < SLOTS
    gate = jnp.tanh(gate_ref[...])
    for h in range(NX):
        sl = slice(h * HD, (h + 1) * HD)
        lkh, lvh, cqh = lks[:, sl], lvs[:, sl], cqv[:, sl]
        raw = dot(lkh, cqh, NT)
        raw = jnp.where(seen, raw * SCALE, BIG)
        w = jnp.where(seen, jnp.exp(raw - jnp.max(raw, axis=0, keepdims=True)), 0.0)
        total = jnp.where(any_image, jnp.sum(w, axis=0, keepdims=True), 1.0)
        probs = w / total
        low = probs.astype(BF16)
        cross[:, sl] = gate[:, sl] * dot(lvh.T, low).T
        back = (gate[:, sl] * dov[:, sl].astype(F32)).astype(BF16)
        gp = dot(lvh, back, NT)
        cdot = jnp.sum(probs * gp, axis=0, keepdims=True)
        ds = (probs * (gp - cdot) * SCALE).astype(BF16)
        cqg_ref[:, sl] = dot(lkh.T, ds).T.astype(cqg_ref.dtype)
        gk[:, sl] = dot(ds, cqh).astype(BF16).astype(F32)
        gv[:, sl] = dot(low, back).astype(BF16).astype(F32)

    for m in range(IMAGES):
        for n, g in enumerate((gk, gv)):
            acc = jnp.zeros((LAT, WD), F32)
            for i in range(SLOTS):
                acc = acc + jnp.where(img_ref[i] == m, 1.0, 0.0) * g[i * LAT:(i + 1) * LAT, :]
            acc = acc.astype(BF16)
            for h in range(2):
                latsend[m // 2, (m % 2) * 2 + h, n] = acc[:, h * 256:(h + 1) * 256]

    def gx_copy(d):
        p = xpeer(d)
        return remote(latsend.at[p], latx.at[d - 1], gx_send.at[d - 1], gx_recv.at[d - 1],
                      z * NX + p, v)

    def gz_copy(d):
        p = zpeer(d)
        return remote(latz.at[p], latzin.at[d - 1], gz_send.at[d - 1], gz_recv.at[d - 1],
                      p * NX + x, v)

    def gp_copy():
        return remote(latp, latin, gp_send.at[0], gp_recv.at[0], to_seq, to_vis)

    for d in ORDER[1:]:
        gx_copy(d).start()

    @pl.when(z >= 1)
    def _():
        z_wait(0, 1)
        z_wait(1, 1)
        forward(1)

    for d in ORDER[1:]:
        landed(latx.at[d - 1], gx_recv.at[d - 1])
    for i in range(NX):
        for n in range(2):
            acc = latsend[x, i, n].astype(F32)
            for d in range(3):
                acc = acc + latx[d, i, n].astype(F32)
            latz[i, n] = acc.astype(BF16)
    for d in ORDER[1:]:
        gz_copy(d).start()

    @pl.when(z >= 2)
    def _():
        z_wait(0, 2)
        z_wait(1, 2)
        forward(0)

    for d in ORDER[1:]:
        a_wait(3, d)

    top = jnp.maximum(jnp.maximum(maxes[0], maxes[1]), maxes[2])
    total = jnp.zeros((1, CH), F32)
    out = jnp.zeros((HD, CH), F32)
    for slot in range(NC):
        factor = jnp.exp2((maxes[slot] - top) * (SCALE * LOG2E))
        maxes[slot] = factor
        total = total + jnp.sum(sums[slot], axis=0, keepdims=True) * factor[0:1]
        out = out + opart[slot] * factor[0:1]
    inv = 1.0 / total
    out = out * inv
    obuf[...] = out.T.astype(BF16)
    dot_t[...] = dobuf[...].astype(F32).T
    row_dot = jnp.sum(dot_t[...] * out, axis=0, keepdims=True)
    for slot in range(NC):
        factor = maxes[slot] * inv
        maxes[slot] = factor
        sums[slot] = factor * row_dot
        dol[slot] = (dot_t[...] * factor[0:1]).T.astype(BF16)
    dqt[...] = jnp.zeros_like(dqt)

    outs = (obuf, dqb, sum_k, sum_v)
    backs = (o_in, dq_in, dk_in, dv_in)

    def b_copy(arr, d):
        p = xpeer(d)
        return remote(outs[arr].at[rows(p), :], backs[arr].at[:, cols(x)],
                      b_send.at[arr, d - 1], b_recv.at[arr, d - 1], z * NX + p, v)

    def b_wait(arr, d):
        landed(backs[arr].at[:, cols(xpeer(NX - d))], b_recv.at[arr, d - 1])

    def b_own(arr):
        backs[arr][:, cols(x)] = outs[arr][rows(x), :]

    for d in ORDER[1:]:
        b_copy(0, d).start()
    b_own(0)

    parts, gots = (part_k, part_v), (got_k, got_v)

    def p_copy(arr, dz, p):
        return remote(parts[arr].at[pl.ds((2 - dz) * CH + p * TD, TD), :],
                      gots[arr].at[pl.ds((dz - 1) * CH + p * TD, TD), :],
                      p_send.at[arr, dz - 1, p], p_recv.at[arr, dz - 1, p], s - dz * NX, v)

    def r_copy(arr, p):
        return remote(parts[arr].at[pl.ds(p * TD, TD), :], stage.at[arr, p],
                      p_send.at[arr, 1, p], f_recv.at[arr, p], s - 3 * NX, v)

    def r_on(arr, p):
        return remote(stage.at[arr, p], gots[arr].at[pl.ds(CH + p * TD, TD), :],
                      f_send.at[arr, p], p_recv.at[arr, 1, p], s + NX, v)

    def p_start(dz, p):
        for arr in (0, 1):
            if dz == 2 and p < 2:
                @pl.when(z == 3)
                def _():
                    r_copy(arr, p).start()

                @pl.when(z == 2)
                def _():
                    p_copy(arr, dz, p).start()
            else:
                p_copy(arr, dz, p).start()

    def backward(slot):
        at = slot * CH
        sent = 0
        for k0, kn, q0, qn in BWD_TILES[slot]:
            down, across = slice(at + k0, at + k0 + kn), slice(q0, q0 + qn)
            pb = pbuf[down, across]
            grad = dol[slot, across, :]
            dp = dot(vbuf[down, :], grad, NT)
            ds = (pb.astype(F32) * (dp - sums[slot, 0:1, across])).astype(BF16)
            dk = dot(ds, qbuf[across, :]) * SCALE
            dv = dot(pb, grad)
            dqt[:, across] += dot(kt[:, down], ds)
            if slot == 2:
                own_k[k0:k0 + kn, :] = dk
                own_v[k0:k0 + kn, :] = dv
            else:
                part_k[down, :] = dk.astype(BF16)
                part_v[down, :] = dv.astype(BF16)
                while (sent + 1) * TD <= k0 + kn:
                    p_start(2 - slot, sent)
                    sent += 1

    @pl.when(z >= 2)
    def _():
        backward(0)

    @pl.when(z >= 1)
    def _():
        backward(1)

    backward(2)
    dqb[...] = (dqt[...] * SCALE).T.astype(BF16)
    for d in ORDER[1:]:
        b_copy(1, d).start()
    b_own(1)

    @pl.when(z == 0)
    def _():
        for p in range(2):
            for arr in (0, 1):
                landed(stage.at[arr, p], f_recv.at[arr, p])
                r_on(arr, p).start()

    for d in ORDER[1:]:
        landed(latzin.at[d - 1], gz_recv.at[d - 1])
    for n in range(2):
        acc = latz[z, n].astype(F32)
        for d in range(3):
            acc = acc + latzin[d, n].astype(F32)
        latp[n] = acc.astype(BF16)

    @pl.when(moves)
    def _():
        gp_copy().start()

    @pl.when(stays)
    def _():
        latin[...] = latp[...]

    for d in ORDER[1:]:
        b_wait(0, d)
    mixed_ref[...] = (o_in[...].astype(F32) + cross[...]).astype(BF16)

    def p_wait(arr, dz, p):
        here = gots[arr].at[pl.ds((dz - 1) * CH + p * TD, TD), :]
        landed(here, p_recv.at[arr, dz - 1, p])
        return here

    for p in range(NX):
        sl = slice(p * TD, (p + 1) * TD)
        for arr, (own, out_) in enumerate(((own_k, sum_k), (own_v, sum_v))):
            for dz in (2, 1):
                @pl.when(z + dz < NX)
                def _():
                    here = p_wait(arr, dz, p)
                    own[sl, :] += here[...].astype(F32)
            out_[sl, :] = own[sl, :].astype(BF16)
        for arr in (2, 3):
            for d in range(1, NX):
                @pl.when(xpeer(d) == p)
                def _():
                    b_copy(arr, d).start()

    @pl.when(moves)
    def _():
        landed(latin, gp_recv.at[0])

    lkg_ref[0] = latin[0].astype(F32)
    lvg_ref[0] = latin[1].astype(F32)
    for d in ORDER[1:]:
        b_wait(1, d)
    qg_ref[...] = dq_in[...]
    for arr, out_ in ((2, kg_ref), (3, vg_ref)):
        b_own(arr)
        for d in ORDER[1:]:
            b_wait(arr, d)
        out_[...] = backs[arr][...]

    for d in range(1, NX):
        for arr in range(4):
            a_copy(arr, d).wait_send()
            b_copy(arr, d).wait_send()
        for step in range(2):
            c_copy(step, d).wait_send()
        gx_copy(d).wait_send()
        gz_copy(d).wait_send()

    @pl.when(moves)
    def _():
        gp_copy().wait_send()

    for arr in (0, 1):
        for d in range(1, IMAGES):
            l_copy(arr, d).wait_send()
        for dz in (1, 2):
            @pl.when(z + dz < NX)
            def _():
                for i in range(NX):
                    z_copy(arr, dz, i).wait_send()

            @pl.when(z >= dz)
            def _():
                for p in range(NX):
                    p_copy(arr, dz, p).wait_send()

        @pl.when(z == 3)
        def _():
            for i in range(2):
                f_on(arr, i).wait_send()

        @pl.when(z == 0)
        def _():
            for p in range(2):
                r_on(arr, p).wait_send()


def widen(mixed_ref, *refs):
    half = len(refs) // 2
    refs[half][...] = mixed_ref[...]
    for src, dst in zip(refs[:half], refs[half + 1:]):
        dst[...] = src[...].astype(F32)


def shards(query, key, value, doc_ids, cross_query, latent_key, latent_value, token_slot,
           slot_image, cross_gate, out_grad):
    vm = pl.BlockSpec(memory_space=pltpu.VMEM)
    sm = pl.BlockSpec(memory_space=pltpu.SMEM)
    hbm = pl.BlockSpec(memory_space=pl.ANY)
    dma = pltpu.SemaphoreType.DMA

    def low(*shape):
        return pltpu.VMEM(shape, BF16)

    def wide(*shape):
        return pltpu.VMEM(shape, F32)

    scratch = [
        low(NC * CH, HD), low(NC * CH, HD), low(CH, HD), low(CH, HD),
        low(NC, CH, HD), low(HD, NC * CH), low(HD, NC * CH),
        wide(CH, CH), low(NC * CH, CH), wide(NC, HD, CH),
        wide(NC, 8, CH), wide(NC, 8, CH), pltpu.VMEM((8, CH), I32),
        wide(HD, CH), wide(HD, CH),
        wide(8, HD), wide(3, 8, HD), wide(8, HD), wide(3, 8, HD),
        low(TD, WD), low(TD, WD), low(2, 2, TD, HD),
        low(IMAGES, LAT, WD), low(IMAGES, LAT, WD),
        low(SLOTS * LAT, WD), low(SLOTS * LAT, WD),
        wide(SLOTS * LAT, WD), wide(SLOTS * LAT, WD), wide(TD, WD),
        low(NX, NX, 2, LAT, 256), low(3, NX, 2, LAT, 256),
        low(NX, 2, LAT, 256), low(3, 2, LAT, 256), low(2, LAT, 256), low(2, LAT, 256),
        low(CH, HD), low(CH, HD), low(2 * CH, HD), low(2 * CH, HD),
        wide(CH, HD), wide(CH, HD), low(2 * CH, HD), low(2 * CH, HD),
        low(CH, HD), low(CH, HD),
        low(TD, WD), low(TD, WD), low(TD, WD), low(TD, WD),
        dma((4, 3)), dma((4, 3)),
        dma((2, 2, 4)), dma((2, 2, 4)),
        dma((2, 3)), dma((2, 3)),
        dma((2, 7)), dma((2, 7)),
        dma((3,)), dma((3,)), dma((3,)), dma((3,)), dma((1,)), dma((1,)),
        dma((2, 2, 4)), dma((2, 2, 4)),
        dma((4, 3)), dma((4, 3)),
        dma((2, 2)), dma((2, 2)), dma((8,)),
    ]
    full = jax.ShapeDtypeStruct((TD, WD), F32)
    half = jax.ShapeDtypeStruct((TD, WD), BF16)
    lat = jax.ShapeDtypeStruct((1, LAT, 256), F32)
    results = pl.pallas_call(
        kernel,
        out_shape=(half,) * 5 + (lat, lat),
        in_specs=[vm, vm, sm, vm] + [hbm] * 7,
        out_specs=(vm,) * 7,
        scratch_shapes=scratch,
        cost_estimate=pl.CostEstimate(flops=6_500_000_000, bytes_accessed=8_000_000, transcendentals=4_000_000),
        compiler_params=pltpu.CompilerParams(
            collective_id=0, has_side_effects=True, vmem_limit_bytes=58 * 1024 * 1024),
    )(
        doc_ids.reshape(1, TD), token_slot.reshape(1, TD), slot_image, cross_gate.reshape(1, WD),
        query, key, value, cross_query, out_grad, latent_key, latent_value,
    )
    return pl.pallas_call(
        widen,
        out_shape=(half,) + (full,) * 4 + (lat, lat),
        in_specs=[vm] * 7,
        out_specs=(vm,) * 7,
        cost_estimate=pl.CostEstimate(flops=1_000_000, bytes_accessed=5_000_000, transcendentals=0),
    )(*results)


def solution(mesh):
    own = P("seq", "vis")
    lat_in = P("vis", None, None)
    lat_out = P("vis", None, "seq")
    return jax.shard_map(
        shards,
        mesh=mesh,
        in_specs=(own, own, own, P("seq"), own, lat_in, lat_in, P("seq"), P("seq"), P("vis"), own),
        out_specs=(own, own, own, own, own, lat_out, lat_out),
        check_vma=False,
    )
```

time: 137 us -> 98.5 us (0.72)
  the two profiles are of different devices: /device:TPU:48 before, /device:TPU:59 now
where the time goes in v2:
time: 98.5 us; the launch traced here: 98.3 us
  Pallas kernels  95.9 us (97%)
  local copies, waits for them, and re-layouts  1.82 us (2%)
    pallas_call x1, Pallas kernels, shards(): pl.pallas_call(kernel, out_shape=(half,) * 5 + (lat, lat), in_specs=[vm,...  92.8 us
    pallas_call x1, Pallas kernels, shards(): pl.pallas_call(widen, out_shape=(half,) + (full,) * 4 + (lat, lat), in_sp...  3.07 us

profile of v2, /device:TPU:59, one launch (start us, length us, event | category | flops | bytes accessed | tf_op | source)
XLA Modules:
  0.0 98.3 jit_solution(8958935512863436356)
XLA Ops:
  0.6 0.0 copy-start
  0.6 1.3 %reshape.23.docs_ref = s32[1,320]{1,0:T(1,128)} reshape(s32[320]{0:T(512)} %param.14) | data formatting | bytes 2560 | tf_op jit(solution)/shard_map/reshape | solution.py:618
  1.9 0.0 copy-done
  1.9 0.6 reshape.24.tok_ref
  2.5 92.8 %shard_map.162 = (bf16[320,512]{1,0:T(8,128)(2,1)}, bf16[320,512]{1,0:T(8,128)(2,1)}, bf16[320,512]{1,0:T(8,128)(2,1)}, bf16[320,512]{1,0:T(8,128)(2,1)}, bf16[3...) custom-call(s32[1,320]{1,0:T(1,128)} %reshape.23.docs_ref, s32[1,320]{1,0:T(1,128)} %reshape.24.tok_ref, ...), custom_call_target="tpu_custom_call" | custom-call | flops 6499999744 | bytes 8000000 | tf_op jit(solution)/shard_map/pallas_call | solution.py:608
  95.3 3.1 %shard_map.163 = (bf16[320,512]{1,0:T(8,128)(2,1)}, f32[320,512]{1,0:T(8,128)}, f32[320,512]{1,0:T(8,128)}, f32[320,512]{1,0:T(8,128)}, f32[320,512]{1,0:T(8,128...) custom-call(bf16[320,512]{1,0:T(8,128)(2,1)} %get-tuple-element.14.mixed_ref, ...), custom_call_target="tpu_custom_call" | custom-call | flops 1000000 | bytes 5000000 | tf_op jit(solution)/shard_map/pallas_call | solution.py:621
Async XLA Ops:
  0.6 1.3 %copy-start = (s32[320]{0:T(512)S(1)}, s32[320]{0:T(512)}, u32[]{:S(2)}) copy-start(s32[320]{0:T(512)} %param.18) | copy-start | bytes 3844

commit v3 on v2

--- a/solution.py
+++ b/solution.py
@@ -1,4 +1,3 @@
-import functools
 import math
 
 import jax
@@ -35,6 +34,7 @@
 def fold(a, op):
     return op(a.reshape(a.shape[0] // 8, 8, a.shape[1]), axis=0)
 
+
 LOG2E = 1.4426950408889634
 
 FWD_TILES = (
@@ -49,10 +49,10 @@
 def kernel(
     docs_ref, tok_ref, img_ref, gate_ref, q_ref, k_ref, v_ref, cq_ref, do_ref, lk_ref, lv_ref,
     mixed_ref, qg_ref, kg_ref, vg_ref, cqg_ref, lkg_ref, lvg_ref,
-    kbuf, vbuf, qbuf, dobuf, dol, kt, vt, sbuf, pbuf, opart, maxes, sums, starts, dot_t, dqt,
+    kbuf, vbuf, qbuf, dobuf, dol, kt, vt, sbuf, pbuf, opart, maxes, sums, dsum, starts, dot_t, dqt,
     cown, cx, crow, cz, cqv, dov, stage,
     latk, latv, lks, lvs, gk, gv, cross, latsend, latx, latz, latzin, latp, latin,
-    obuf, dqb, part_k, part_v, own_k, own_v, got_k, got_v, sum_k, sum_v,
+    obuf, dqb, part_k, part_v, sum_k, sum_v, lands,
     o_in, dq_in, dk_in, dv_in,
     a_send, a_recv, z_send, z_recv, c_send, c_recv, l_send, l_recv, gx_send, gx_recv, gz_send, gz_recv,
     gp_send, gp_recv, p_send, p_recv, b_send, b_recv, f_send, f_recv, own_sem,
@@ -98,9 +98,10 @@
     stays = jnp.logical_and(to_seq == s, to_vis == v)
     moves = jnp.logical_not(stays)
 
-    for d in range(1, NX):
-        greet(z * NX + xpeer(d), v)
-        greet(zpeer(d) * NX + x, v)
+    for dz in range(NX):
+        for d in range(NX):
+            if dz or d:
+                greet(zpeer(dz) * NX + xpeer(d), v)
     for d in range(1, IMAGES):
         greet(s, lax.rem(v + d, IMAGES))
 
@@ -124,14 +125,14 @@
     for i in range(8):
         own_copy(i).start()
 
-    docs = docs_ref[...]
+    docs = docs_ref[...].reshape(1, TD)
     row_id = lax.broadcasted_iota(I32, (8, HD), 0)
     counts = jnp.zeros((8, HD), F32)
     for d in range(1, 4):
         c = jnp.sum(jnp.where(docs < d, 1.0, 0.0), axis=1, keepdims=True)
         counts = jnp.where(row_id == d, c, counts)
     cown[...] = counts
-    pl.semaphore_wait(barrier, 13 + jnp.where(stays, 0, 1))
+    pl.semaphore_wait(barrier, 22 + jnp.where(stays, 0, 1))
 
     ins = (k_ref, v_ref, q_ref, do_ref)
     bufs = (kbuf, vbuf, qbuf, dobuf)
@@ -273,7 +274,16 @@
             sums[slot, :, across] += fold(p, jnp.sum)
             opart[slot, :, across] += dot(vt[:, at + k0:at + k0 + kn], pb)
 
+    def row_sum(slot):
+        dsum[slot] = jnp.broadcast_to(jnp.sum(dot_t[...] * opart[slot], axis=0, keepdims=True), (8, CH))
+
+    dsum[0] = jnp.zeros((8, CH), F32)
+    dsum[1] = jnp.zeros((8, CH), F32)
     forward(2)
+    for d in ORDER[1:]:
+        a_wait(3, d)
+    dot_t[...] = dobuf[...].astype(F32).T
+    row_sum(2)
 
     for arr in (0, 1):
         for d in range(1, IMAGES):
@@ -282,9 +292,10 @@
         lks[i * LAT:(i + 1) * LAT, :] = latk[img_ref[i]]
         lvs[i * LAT:(i + 1) * LAT, :] = latv[img_ref[i]]
     slot_of = lax.broadcasted_iota(I32, (SLOTS * LAT, TD), 0) // LAT
-    seen = slot_of == tok_ref[...]
-    any_image = tok_ref[...] < SLOTS
-    gate = jnp.tanh(gate_ref[...])
+    toks = tok_ref[...].reshape(1, TD)
+    seen = slot_of == toks
+    any_image = toks < SLOTS
+    gate = jnp.tanh(gate_ref[...].reshape(1, WD))
     for h in range(NX):
         sl = slice(h * HD, (h + 1) * HD)
         lkh, lvh, cqh = lks[:, sl], lvs[:, sl], cqv[:, sl]
@@ -333,6 +344,7 @@
         z_wait(0, 1)
         z_wait(1, 1)
         forward(1)
+        row_sum(1)
 
     for d in ORDER[1:]:
         landed(latx.at[d - 1], gx_recv.at[d - 1])
@@ -350,29 +362,39 @@
         z_wait(0, 2)
         z_wait(1, 2)
         forward(0)
-
-    for d in ORDER[1:]:
-        a_wait(3, d)
+        row_sum(0)
 
     top = jnp.maximum(jnp.maximum(maxes[0], maxes[1]), maxes[2])
     total = jnp.zeros((1, CH), F32)
-    out = jnp.zeros((HD, CH), F32)
+    row_dot = jnp.zeros((8, CH), F32)
     for slot in range(NC):
         factor = jnp.exp2((maxes[slot] - top) * (SCALE * LOG2E))
         maxes[slot] = factor
         total = total + jnp.sum(sums[slot], axis=0, keepdims=True) * factor[0:1]
-        out = out + opart[slot] * factor[0:1]
+        row_dot = row_dot + dsum[slot] * factor
     inv = 1.0 / total
-    out = out * inv
-    obuf[...] = out.T.astype(BF16)
-    dot_t[...] = dobuf[...].astype(F32).T
-    row_dot = jnp.sum(dot_t[...] * out, axis=0, keepdims=True)
+    row_dot = row_dot * inv
     for slot in range(NC):
         factor = maxes[slot] * inv
         maxes[slot] = factor
         sums[slot] = factor * row_dot
-        dol[slot] = (dot_t[...] * factor[0:1]).T.astype(BF16)
     dqt[...] = jnp.zeros_like(dqt)
+
+    for d in ORDER[1:]:
+        landed(latzin.at[d - 1], gz_recv.at[d - 1])
+    for n in range(2):
+        acc = latz[z, n].astype(F32)
+        for d in range(3):
+            acc = acc + latzin[d, n].astype(F32)
+        latp[n] = acc.astype(BF16)
+
+    @pl.when(moves)
+    def _():
+        gp_copy().start()
+
+    @pl.when(stays)
+    def _():
+        latin[...] = latp[...]
 
     outs = (obuf, dqb, sum_k, sum_v)
     backs = (o_in, dq_in, dk_in, dv_in)
@@ -388,33 +410,31 @@
     def b_own(arr):
         backs[arr][:, cols(x)] = outs[arr][rows(x), :]
 
-    for d in ORDER[1:]:
-        b_copy(0, d).start()
-    b_own(0)
-
-    parts, gots = (part_k, part_v), (got_k, got_v)
+    parts = (part_k, part_v)
 
     def p_copy(arr, dz, p):
-        return remote(parts[arr].at[pl.ds((2 - dz) * CH + p * TD, TD), :],
-                      gots[arr].at[pl.ds((dz - 1) * CH + p * TD, TD), :],
-                      p_send.at[arr, dz - 1, p], p_recv.at[arr, dz - 1, p], s - dz * NX, v)
-
-    def r_copy(arr, p):
-        return remote(parts[arr].at[pl.ds(p * TD, TD), :], stage.at[arr, p],
-                      p_send.at[arr, 1, p], f_recv.at[arr, p], s - 3 * NX, v)
-
-    def r_on(arr, p):
-        return remote(stage.at[arr, p], gots[arr].at[pl.ds(CH + p * TD, TD), :],
-                      f_send.at[arr, p], p_recv.at[arr, 1, p], s + NX, v)
+        return remote(parts[arr].at[piece(2 - dz, p), :], lands.at[dz - 1, arr, :, cols(x)],
+                      p_send.at[arr, dz - 1, p], p_recv.at[arr, dz - 1, x], (z - dz) * NX + p, v)
+
+    def r_copy(arr, p, d):
+        return remote(parts[arr].at[piece(0, p), :], stage.at[arr, d],
+                      p_send.at[arr, 1, p], f_recv.at[arr, d], x, v)
+
+    def r_on(arr, d):
+        return remote(stage.at[arr, d], lands.at[1, arr, :, cols(x)],
+                      f_send.at[arr, d], p_recv.at[arr, 1, x], NX + xpeer(d), v)
 
     def p_start(dz, p):
+        d = lax.rem(p - x + NX, NX)
         for arr in (0, 1):
-            if dz == 2 and p < 2:
-                @pl.when(z == 3)
+            if dz == 2:
+                around = jnp.logical_and(z == 3, d < 2)
+
+                @pl.when(around)
                 def _():
-                    r_copy(arr, p).start()
-
-                @pl.when(z == 2)
+                    r_copy(arr, p, d).start()
+
+                @pl.when(jnp.logical_not(around))
                 def _():
                     p_copy(arr, dz, p).start()
             else:
@@ -423,6 +443,7 @@
     def backward(slot):
         at = slot * CH
         sent = 0
+        dol[slot] = (dot_t[...] * maxes[slot, 0:1, :]).T.astype(BF16)
         for k0, kn, q0, qn in BWD_TILES[slot]:
             down, across = slice(at + k0, at + k0 + kn), slice(q0, q0 + qn)
             pb = pbuf[down, across]
@@ -433,8 +454,8 @@
             dv = dot(pb, grad)
             dqt[:, across] += dot(kt[:, down], ds)
             if slot == 2:
-                own_k[k0:k0 + kn, :] = dk
-                own_v[k0:k0 + kn, :] = dv
+                sum_k[k0:k0 + kn, :] = dk.astype(BF16)
+                sum_v[k0:k0 + kn, :] = dv.astype(BF16)
             else:
                 part_k[down, :] = dk.astype(BF16)
                 part_v[down, :] = dv.astype(BF16)
@@ -450,7 +471,16 @@
     def _():
         backward(1)
 
+    out = opart[0] * maxes[0, 0:1, :] + opart[1] * maxes[1, 0:1, :] + opart[2] * maxes[2, 0:1, :]
+    obuf[...] = out.T.astype(BF16)
+    for d in ORDER[1:]:
+        b_copy(0, d).start()
+    b_own(0)
     backward(2)
+    for arr in (2, 3):
+        for d in ORDER[1:]:
+            b_copy(arr, d).start()
+        b_own(arr)
     dqb[...] = (dqt[...] * SCALE).T.astype(BF16)
     for d in ORDER[1:]:
         b_copy(1, d).start()
@@ -458,51 +488,15 @@
 
     @pl.when(z == 0)
     def _():
-        for p in range(2):
+        for d in range(2):
             for arr in (0, 1):
-                landed(stage.at[arr, p], f_recv.at[arr, p])
-                r_on(arr, p).start()
-
-    for d in ORDER[1:]:
-        landed(latzin.at[d - 1], gz_recv.at[d - 1])
-    for n in range(2):
-        acc = latz[z, n].astype(F32)
-        for d in range(3):
-            acc = acc + latzin[d, n].astype(F32)
-        latp[n] = acc.astype(BF16)
-
-    @pl.when(moves)
-    def _():
-        gp_copy().start()
-
-    @pl.when(stays)
-    def _():
-        latin[...] = latp[...]
+                landed(stage.at[arr, d], f_recv.at[arr, d])
+                r_on(arr, d).start()
 
     for d in ORDER[1:]:
         b_wait(0, d)
     mixed_ref[...] = (o_in[...].astype(F32) + cross[...]).astype(BF16)
 
-    def p_wait(arr, dz, p):
-        here = gots[arr].at[pl.ds((dz - 1) * CH + p * TD, TD), :]
-        landed(here, p_recv.at[arr, dz - 1, p])
-        return here
-
-    for p in range(NX):
-        sl = slice(p * TD, (p + 1) * TD)
-        for arr, (own, out_) in enumerate(((own_k, sum_k), (own_v, sum_v))):
-            for dz in (2, 1):
-                @pl.when(z + dz < NX)
-                def _():
-                    here = p_wait(arr, dz, p)
-                    own[sl, :] += here[...].astype(F32)
-            out_[sl, :] = own[sl, :].astype(BF16)
-        for arr in (2, 3):
-            for d in range(1, NX):
-                @pl.when(xpeer(d) == p)
-                def _():
-                    b_copy(arr, d).start()
-
     @pl.when(moves)
     def _():
         landed(latin, gp_recv.at[0])
@@ -512,11 +506,30 @@
     for d in ORDER[1:]:
         b_wait(1, d)
     qg_ref[...] = dq_in[...]
-    for arr, out_ in ((2, kg_ref), (3, vg_ref)):
-        b_own(arr)
+
+    def p_wait(arr, dz):
+        for p in range(NX):
+            landed(lands.at[dz - 1, arr, :, pl.ds(p * HD, HD)], p_recv.at[arr, dz - 1, p])
+
+    for arr, out_ in ((0, kg_ref), (1, vg_ref)):
         for d in ORDER[1:]:
-            b_wait(arr, d)
-        out_[...] = backs[arr][...]
+            b_wait(arr + 2, d)
+
+        @pl.when(z == 3)
+        def _():
+            out_[...] = backs[arr + 2][...]
+
+        @pl.when(z == 2)
+        def _():
+            p_wait(arr, 1)
+            out_[...] = (backs[arr + 2][...].astype(F32) + lands[0, arr].astype(F32)).astype(BF16)
+
+        @pl.when(z < 2)
+        def _():
+            p_wait(arr, 1)
+            p_wait(arr, 2)
+            out_[...] = (backs[arr + 2][...].astype(F32) + lands[0, arr].astype(F32)
+                         + lands[1, arr].astype(F32)).astype(BF16)
 
     for d in range(1, NX):
         for arr in range(4):
@@ -580,7 +593,7 @@
         low(NC * CH, HD), low(NC * CH, HD), low(CH, HD), low(CH, HD),
         low(NC, CH, HD), low(HD, NC * CH), low(HD, NC * CH),
         wide(CH, CH), low(NC * CH, CH), wide(NC, HD, CH),
-        wide(NC, 8, CH), wide(NC, 8, CH), pltpu.VMEM((8, CH), I32),
+        wide(NC, 8, CH), wide(NC, 8, CH), wide(NC, 8, CH), pltpu.VMEM((8, CH), I32),
         wide(HD, CH), wide(HD, CH),
         wide(8, HD), wide(3, 8, HD), wide(8, HD), wide(3, 8, HD),
         low(TD, WD), low(TD, WD), low(2, 2, TD, HD),
@@ -590,8 +603,7 @@
         low(NX, NX, 2, LAT, 256), low(3, NX, 2, LAT, 256),
         low(NX, 2, LAT, 256), low(3, 2, LAT, 256), low(2, LAT, 256), low(2, LAT, 256),
         low(CH, HD), low(CH, HD), low(2 * CH, HD), low(2 * CH, HD),
-        wide(CH, HD), wide(CH, HD), low(2 * CH, HD), low(2 * CH, HD),
-        low(CH, HD), low(CH, HD),
+        low(CH, HD), low(CH, HD), low(2, 2, TD, WD),
         low(TD, WD), low(TD, WD), low(TD, WD), low(TD, WD),
         dma((4, 3)), dma((4, 3)),
         dma((2, 2, 4)), dma((2, 2, 4)),
@@ -613,9 +625,9 @@
         scratch_shapes=scratch,
         cost_estimate=pl.CostEstimate(flops=6_500_000_000, bytes_accessed=8_000_000, transcendentals=4_000_000),
         compiler_params=pltpu.CompilerParams(
-            collective_id=0, has_side_effects=True, vmem_limit_bytes=58 * 1024 * 1024),
+            collective_id=0, has_side_effects=True, vmem_limit_bytes=52 * 1024 * 1024),
     )(
-        doc_ids.reshape(1, TD), token_slot.reshape(1, TD), slot_image, cross_gate.reshape(1, WD),
+        doc_ids, token_slot, slot_image, cross_gate,
         query, key, value, cross_query, out_grad, latent_key, latent_value,
     )
     return pl.pallas_call(

time: 98.5 us -> 99.4 us (level)
  the two profiles are of different devices: /device:TPU:59 before, /device:TPU:118 now
where the time goes in v3:
time: 99.4 us; the launch traced here: 99.2 us
  Pallas kernels  91 us (92%)
  local copies, waits for them, and re-layouts  7.54 us (8%)
    pallas_call x1, Pallas kernels, shards(): pl.pallas_call(kernel, out_shape=(half,) * 5 + (lat, lat), in_specs=[vm,...  87.9 us
    unnamed x22, local copies, waits for them, and re-layouts  7.54 us
    pallas_call x1, Pallas kernels, shards(): pl.pallas_call(widen, out_shape=(half,) + (full,) * 4 + (lat, lat), in_sp...  3.07 us

profile of v3, /device:TPU:118, one launch (start us, length us, event | category | flops | bytes accessed | tf_op | source)
XLA Modules:
  0.0 99.2 jit_solution(4680468968316931348)
XLA Ops:
  0.6 0.0 copy-start.7
  0.6 0.7 copy-done.7
  1.3 0.0 copy-start.8
  1.3 0.7 copy-done.8
  2.0 0.0 copy-start.9
  2.0 0.7 copy-done.9
  2.7 0.0 copy-start.10
  2.7 0.7 copy-done.10
  3.3 87.9 %shard_map.162 = (bf16[320,512]{1,0:T(8,128)(2,1)S(1)}, bf16[320,512]{1,0:T(8,128)(2,1)S(1)}, bf16[320,512]{1,0:T(8,128)(2,1)S(1)}, bf16[320,512]{1,0:T(8,128)(2...) custom-call(s32[320]{0:T(512)S(1)} %copy-done.7, s32[320]{0:T(512)S(1)} %copy-done.8, ...), custom_call_target="tpu_custom_call" | custom-call | flops 6499999744 | bytes 8000000 | tf_op jit(solution)/shard_map/pallas_call | solution.py:620
  91.3 0.0 copy-start
  91.3 0.7 copy-done
  92.0 0.0 copy-start.1
  92.0 0.7 copy-done.1
  92.7 0.0 copy-start.2
  92.7 0.7 copy-done.2
  93.4 0.0 copy-start.3
  93.4 0.7 copy-done.3
  94.2 0.0 copy-start.4
  94.2 0.7 copy-done.4
  94.9 0.0 copy-start.5
  94.9 0.6 copy-done.5
  95.5 0.0 copy-start.6
  95.5 0.6 copy-done.6
  96.1 3.1 %shard_map.163 = (bf16[320,512]{1,0:T(8,128)(2,1)}, f32[320,512]{1,0:T(8,128)}, f32[320,512]{1,0:T(8,128)}, f32[320,512]{1,0:T(8,128)}, f32[320,512]{1,0:T(8,128...) custom-call(bf16[320,512]{1,0:T(8,128)(2,1)} %copy-done, bf16[320,512]{1,0:T(8,128)(2,1)} %copy-done.1, ...), custom_call_target="tpu_custom_call" | custom-call | flops 1000000 | bytes 5000000 | tf_op jit(solution)/shard_map/pallas_call | solution.py:633
Async XLA Ops:
  0.6 0.7 copy-start.7
  1.3 0.7 copy-start.8
  2.0 0.7 copy-start.9
  2.7 0.7 copy-start.10
  91.3 0.7 copy-start
  92.0 0.7 copy-start.1
  92.7 0.7 copy-start.2
  93.4 0.7 copy-start.3
  94.2 0.7 copy-start.4
  94.9 0.6 copy-start.5
  95.5 0.6 copy-start.6

commit v4 on v2

--- a/solution.py
+++ b/solution.py
@@ -1,4 +1,3 @@
-import functools
 import math
 
 import jax
@@ -35,6 +34,7 @@
 def fold(a, op):
     return op(a.reshape(a.shape[0] // 8, 8, a.shape[1]), axis=0)
 
+
 LOG2E = 1.4426950408889634
 
 FWD_TILES = (
@@ -49,18 +49,19 @@
 def kernel(
     docs_ref, tok_ref, img_ref, gate_ref, q_ref, k_ref, v_ref, cq_ref, do_ref, lk_ref, lv_ref,
     mixed_ref, qg_ref, kg_ref, vg_ref, cqg_ref, lkg_ref, lvg_ref,
-    kbuf, vbuf, qbuf, dobuf, dol, kt, vt, sbuf, pbuf, opart, maxes, sums, starts, dot_t, dqt,
+    kbuf, vbuf, qbuf, dobuf, dol, kt, vt, sbuf, pbuf, opart, maxes, sums, dsum, starts, dot_t, dqt,
     cown, cx, crow, cz, cqv, dov, stage,
-    latk, latv, lks, lvs, gk, gv, cross, latsend, latx, latz, latzin, latp, latin,
+    latk, latv, lks, lvs, gk, gv, cross, latsend, latx, latz, latin,
     obuf, dqb, part_k, part_v, own_k, own_v, got_k, got_v, sum_k, sum_v,
     o_in, dq_in, dk_in, dv_in,
     a_send, a_recv, z_send, z_recv, c_send, c_recv, l_send, l_recv, gx_send, gx_recv, gz_send, gz_recv,
-    gp_send, gp_recv, p_send, p_recv, b_send, b_recv, f_send, f_recv, own_sem,
+    p_send, p_recv, b_send, b_recv, f_send, f_recv, own_sem,
 ):
     s = lax.axis_index("seq")
     v = lax.axis_index("vis")
     x = lax.rem(s, NX)
     z = lax.div(s, NX)
+    core = lax.rem(v, 2)
 
     def xpeer(d):
         return lax.rem(x + d, NX)
@@ -91,12 +92,22 @@
     def greet(seq, vis):
         pl.semaphore_signal(barrier, inc=1, device_id=(seq, vis), device_id_type=MESH)
 
-    to_seq = 2 * v + lax.rem(z, 2)
-    to_vis = 2 * x + lax.div(z, 2)
-    from_seq = (2 * lax.rem(v, 2) + lax.rem(s, 2)) * NX + lax.div(v, 2)
+    def to_seq(j):
+        return 2 * v + j % 2
+
+    def to_vis(j):
+        return 2 * x + j // 2
+
+    def stays(j):
+        return jnp.logical_and(to_seq(j) == s, to_vis(j) == v)
+
+    def from_seq(i):
+        return i * NX + lax.div(v, 2)
+
     from_vis = lax.div(s, 2)
-    stays = jnp.logical_and(to_seq == s, to_vis == v)
-    moves = jnp.logical_not(stays)
+
+    def from_self(i):
+        return jnp.logical_and(from_seq(i) == s, from_vis == v)
 
     for d in range(1, NX):
         greet(z * NX + xpeer(d), v)
@@ -104,9 +115,10 @@
     for d in range(1, IMAGES):
         greet(s, lax.rem(v + d, IMAGES))
 
-    @pl.when(moves)
-    def _():
-        greet(from_seq, from_vis)
+    for i in range(NX):
+        @pl.when(jnp.logical_not(from_self(i)))
+        def _():
+            greet(from_seq(i), from_vis)
 
     def own_copy(i):
         src, dst = (
@@ -124,14 +136,14 @@
     for i in range(8):
         own_copy(i).start()
 
-    docs = docs_ref[...]
+    docs = docs_ref[...].reshape(1, TD)
     row_id = lax.broadcasted_iota(I32, (8, HD), 0)
     counts = jnp.zeros((8, HD), F32)
     for d in range(1, 4):
         c = jnp.sum(jnp.where(docs < d, 1.0, 0.0), axis=1, keepdims=True)
         counts = jnp.where(row_id == d, c, counts)
     cown[...] = counts
-    pl.semaphore_wait(barrier, 13 + jnp.where(stays, 0, 1))
+    pl.semaphore_wait(barrier, 13 + NX - sum(jnp.where(stays(j), 1, 0) for j in range(NX)))
 
     ins = (k_ref, v_ref, q_ref, do_ref)
     bufs = (kbuf, vbuf, qbuf, dobuf)
@@ -197,15 +209,30 @@
         for i in range(NX):
             landed(bufs[arr].at[piece(2 - dz, xpeer(NX - ORDER[i])), :], z_recv.at[arr, dz - 1, i])
 
-    for arr in (0, 1):
-        z_start(arr, 0)
+    def a_start(arr):
+        if arr < 2:
+            z_start(arr, 0)
         for d in ORDER[1:]:
             a_copy(arr, d).start()
+
+    def a_finish(arr):
+        for i in range(1, NX):
+            a_wait(arr, ORDER[i])
+            if arr < 2:
+                z_start(arr, i)
+
+    @pl.when(core == 0)
+    def _():
+        for arr in (0, 1, 2):
+            a_start(arr)
+
+    @pl.when(core == 1)
+    def _():
+        for arr in (2, 3):
+            a_start(arr)
+
     for d in ORDER[1:]:
         c_copy(0, d).start()
-    for arr in (2, 3):
-        for d in ORDER[1:]:
-            a_copy(arr, d).start()
 
     lins, lbufs = (lk_ref, lv_ref), (latk, latv)
 
@@ -218,10 +245,21 @@
         for d in range(1, IMAGES):
             l_copy(arr, d).start()
 
-    for arr in (0, 1):
-        for i in range(1, NX):
-            a_wait(arr, ORDER[i])
-            z_start(arr, i)
+    @pl.when(core == 0)
+    def _():
+        a_finish(0)
+        a_finish(1)
+        a_start(3)
+
+    @pl.when(core == 1)
+    def _():
+        a_finish(2)
+        a_finish(3)
+        a_start(0)
+        a_start(1)
+        a_finish(0)
+        a_finish(1)
+
     f_relay(0)
 
     for d in ORDER[1:]:
@@ -231,9 +269,12 @@
         c_copy(1, d).start()
     for i in range(8):
         own_copy(i).wait()
-    for d in ORDER[1:]:
-        a_wait(2, d)
     f_relay(1)
+
+    @pl.when(core == 0)
+    def _():
+        a_finish(2)
+
     for d in range(1, NX):
         landed(cz.at[d - 1], c_recv.at[1, d - 1])
     before = crow[...] + cz[0] + cz[1] + cz[2]
@@ -273,7 +314,19 @@
             sums[slot, :, across] += fold(p, jnp.sum)
             opart[slot, :, across] += dot(vt[:, at + k0:at + k0 + kn], pb)
 
+    def row_sum(slot):
+        dsum[slot] = jnp.broadcast_to(jnp.sum(dot_t[...] * opart[slot], axis=0, keepdims=True), (8, CH))
+
+    dsum[0] = jnp.zeros((8, CH), F32)
+    dsum[1] = jnp.zeros((8, CH), F32)
     forward(2)
+
+    @pl.when(core == 0)
+    def _():
+        a_finish(3)
+
+    dot_t[...] = dobuf[...].astype(F32).T
+    row_sum(2)
 
     for arr in (0, 1):
         for d in range(1, IMAGES):
@@ -282,9 +335,10 @@
         lks[i * LAT:(i + 1) * LAT, :] = latk[img_ref[i]]
         lvs[i * LAT:(i + 1) * LAT, :] = latv[img_ref[i]]
     slot_of = lax.broadcasted_iota(I32, (SLOTS * LAT, TD), 0) // LAT
-    seen = slot_of == tok_ref[...]
-    any_image = tok_ref[...] < SLOTS
-    gate = jnp.tanh(gate_ref[...])
+    toks = tok_ref[...].reshape(1, TD)
+    seen = slot_of == toks
+    any_image = toks < SLOTS
+    gate = jnp.tanh(gate_ref[...].reshape(1, WD))
     for h in range(NX):
         sl = slice(h * HD, (h + 1) * HD)
         lkh, lvh, cqh = lks[:, sl], lvs[:, sl], cqv[:, sl]
@@ -317,13 +371,8 @@
         return remote(latsend.at[p], latx.at[d - 1], gx_send.at[d - 1], gx_recv.at[d - 1],
                       z * NX + p, v)
 
-    def gz_copy(d):
-        p = zpeer(d)
-        return remote(latz.at[p], latzin.at[d - 1], gz_send.at[d - 1], gz_recv.at[d - 1],
-                      p * NX + x, v)
-
-    def gp_copy():
-        return remote(latp, latin, gp_send.at[0], gp_recv.at[0], to_seq, to_vis)
+    def gz_copy(j):
+        return remote(latz.at[j], latin.at[z], gz_send.at[j], gz_recv.at[z], to_seq(j), to_vis(j))
 
     for d in ORDER[1:]:
         gx_copy(d).start()
@@ -333,45 +382,29 @@
         z_wait(0, 1)
         z_wait(1, 1)
         forward(1)
-
-    for d in ORDER[1:]:
-        landed(latx.at[d - 1], gx_recv.at[d - 1])
-    for i in range(NX):
-        for n in range(2):
-            acc = latsend[x, i, n].astype(F32)
-            for d in range(3):
-                acc = acc + latx[d, i, n].astype(F32)
-            latz[i, n] = acc.astype(BF16)
-    for d in ORDER[1:]:
-        gz_copy(d).start()
+        row_sum(1)
 
     @pl.when(z >= 2)
     def _():
         z_wait(0, 2)
         z_wait(1, 2)
         forward(0)
-
-    for d in ORDER[1:]:
-        a_wait(3, d)
+        row_sum(0)
 
     top = jnp.maximum(jnp.maximum(maxes[0], maxes[1]), maxes[2])
     total = jnp.zeros((1, CH), F32)
-    out = jnp.zeros((HD, CH), F32)
+    row_dot = jnp.zeros((8, CH), F32)
     for slot in range(NC):
         factor = jnp.exp2((maxes[slot] - top) * (SCALE * LOG2E))
         maxes[slot] = factor
         total = total + jnp.sum(sums[slot], axis=0, keepdims=True) * factor[0:1]
-        out = out + opart[slot] * factor[0:1]
+        row_dot = row_dot + dsum[slot] * factor
     inv = 1.0 / total
-    out = out * inv
-    obuf[...] = out.T.astype(BF16)
-    dot_t[...] = dobuf[...].astype(F32).T
-    row_dot = jnp.sum(dot_t[...] * out, axis=0, keepdims=True)
+    row_dot = row_dot * inv
     for slot in range(NC):
         factor = maxes[slot] * inv
         maxes[slot] = factor
         sums[slot] = factor * row_dot
-        dol[slot] = (dot_t[...] * factor[0:1]).T.astype(BF16)
     dqt[...] = jnp.zeros_like(dqt)
 
     outs = (obuf, dqb, sum_k, sum_v)
@@ -388,10 +421,6 @@
     def b_own(arr):
         backs[arr][:, cols(x)] = outs[arr][rows(x), :]
 
-    for d in ORDER[1:]:
-        b_copy(0, d).start()
-    b_own(0)
-
     parts, gots = (part_k, part_v), (got_k, got_v)
 
     def p_copy(arr, dz, p):
@@ -401,11 +430,11 @@
 
     def r_copy(arr, p):
         return remote(parts[arr].at[pl.ds(p * TD, TD), :], stage.at[arr, p],
-                      p_send.at[arr, 1, p], f_recv.at[arr, p], s - 3 * NX, v)
+                      p_send.at[arr, 1, p], f_recv.at[arr, p], x, v)
 
     def r_on(arr, p):
         return remote(stage.at[arr, p], gots[arr].at[pl.ds(CH + p * TD, TD), :],
-                      f_send.at[arr, p], p_recv.at[arr, 1, p], s + NX, v)
+                      f_send.at[arr, p], p_recv.at[arr, 1, p], NX + x, v)
 
     def p_start(dz, p):
         for arr in (0, 1):
@@ -423,6 +452,7 @@
     def backward(slot):
         at = slot * CH
         sent = 0
+        dol[slot] = (dot_t[...] * maxes[slot, 0:1, :]).T.astype(BF16)
         for k0, kn, q0, qn in BWD_TILES[slot]:
             down, across = slice(at + k0, at + k0 + kn), slice(q0, q0 + qn)
             pb = pbuf[down, across]
@@ -446,10 +476,32 @@
     def _():
         backward(0)
 
+    for d in ORDER[1:]:
+        landed(latx.at[d - 1], gx_recv.at[d - 1])
+    for j in range(NX):
+        for n in range(2):
+            acc = latsend[x, j, n].astype(F32)
+            for d in range(3):
+                acc = acc + latx[d, j, n].astype(F32)
+            latz[j, n] = acc.astype(BF16)
+
+        @pl.when(jnp.logical_not(stays(j)))
+        def _():
+            gz_copy(j).start()
+
+        @pl.when(stays(j))
+        def _():
+            latin[z] = latz[j]
+
     @pl.when(z >= 1)
     def _():
         backward(1)
 
+    out = opart[0] * maxes[0, 0:1, :] + opart[1] * maxes[1, 0:1, :] + opart[2] * maxes[2, 0:1, :]
+    obuf[...] = out.T.astype(BF16)
+    for d in ORDER[1:]:
+        b_copy(0, d).start()
+    b_own(0)
     backward(2)
     dqb[...] = (dqt[...] * SCALE).T.astype(BF16)
     for d in ORDER[1:]:
@@ -462,26 +514,6 @@
             for arr in (0, 1):
                 landed(stage.at[arr, p], f_recv.at[arr, p])
                 r_on(arr, p).start()
-
-    for d in ORDER[1:]:
-        landed(latzin.at[d - 1], gz_recv.at[d - 1])
-    for n in range(2):
-        acc = latz[z, n].astype(F32)
-        for d in range(3):
-            acc = acc + latzin[d, n].astype(F32)
-        latp[n] = acc.astype(BF16)
-
-    @pl.when(moves)
-    def _():
-        gp_copy().start()
-
-    @pl.when(stays)
-    def _():
-        latin[...] = latp[...]
-
-    for d in ORDER[1:]:
-        b_wait(0, d)
-    mixed_ref[...] = (o_in[...].astype(F32) + cross[...]).astype(BF16)
 
     def p_wait(arr, dz, p):
         here = gots[arr].at[pl.ds((dz - 1) * CH + p * TD, TD), :]
@@ -497,21 +529,31 @@
                     here = p_wait(arr, dz, p)
                     own[sl, :] += here[...].astype(F32)
             out_[sl, :] = own[sl, :].astype(BF16)
-        for arr in (2, 3):
-            for d in range(1, NX):
-                @pl.when(xpeer(d) == p)
-                def _():
-                    b_copy(arr, d).start()
-
-    @pl.when(moves)
-    def _():
-        landed(latin, gp_recv.at[0])
-
-    lkg_ref[0] = latin[0].astype(F32)
-    lvg_ref[0] = latin[1].astype(F32)
+
+            @pl.when(x != p)
+            def _():
+                d = lax.rem(p - x + NX, NX)
+                remote(out_.at[sl, :], backs[arr + 2].at[:, cols(x)],
+                       b_send.at[arr + 2, d - 1], b_recv.at[arr + 2, d - 1], z * NX + p, v).start()
+
+    for d in ORDER[1:]:
+        b_wait(0, d)
+    mixed_ref[...] = (o_in[...].astype(F32) + cross[...]).astype(BF16)
+
+    for i in range(NX):
+        @pl.when(jnp.logical_not(from_self(i)))
+        def _():
+            landed(latin.at[i], gz_recv.at[i])
+
+    for n, g in enumerate((lkg_ref, lvg_ref)):
+        acc = latin[0, n].astype(F32)
+        for i in range(1, NX):
+            acc = acc + latin[i, n].astype(F32)
+        g[0] = acc
     for d in ORDER[1:]:
         b_wait(1, d)
     qg_ref[...] = dq_in[...]
+
     for arr, out_ in ((2, kg_ref), (3, vg_ref)):
         b_own(arr)
         for d in ORDER[1:]:
@@ -525,11 +567,11 @@
         for step in range(2):
             c_copy(step, d).wait_send()
         gx_copy(d).wait_send()
-        gz_copy(d).wait_send()
-
-    @pl.when(moves)
-    def _():
-        gp_copy().wait_send()
+
+    for j in range(NX):
+        @pl.when(jnp.logical_not(stays(j)))
+        def _():
+            gz_copy(j).wait_send()
 
     for arr in (0, 1):
         for d in range(1, IMAGES):
@@ -580,7 +622,7 @@
         low(NC * CH, HD), low(NC * CH, HD), low(CH, HD), low(CH, HD),
         low(NC, CH, HD), low(HD, NC * CH), low(HD, NC * CH),
         wide(CH, CH), low(NC * CH, CH), wide(NC, HD, CH),
-        wide(NC, 8, CH), wide(NC, 8, CH), pltpu.VMEM((8, CH), I32),
+        wide(NC, 8, CH), wide(NC, 8, CH), wide(NC, 8, CH), pltpu.VMEM((8, CH), I32),
         wide(HD, CH), wide(HD, CH),
         wide(8, HD), wide(3, 8, HD), wide(8, HD), wide(3, 8, HD),
         low(TD, WD), low(TD, WD), low(2, 2, TD, HD),
@@ -588,7 +630,7 @@
         low(SLOTS * LAT, WD), low(SLOTS * LAT, WD),
         wide(SLOTS * LAT, WD), wide(SLOTS * LAT, WD), wide(TD, WD),
         low(NX, NX, 2, LAT, 256), low(3, NX, 2, LAT, 256),
-        low(NX, 2, LAT, 256), low(3, 2, LAT, 256), low(2, LAT, 256), low(2, LAT, 256),
+        low(NX, 2, LAT, 256), low(NX, 2, LAT, 256),
         low(CH, HD), low(CH, HD), low(2 * CH, HD), low(2 * CH, HD),
         wide(CH, HD), wide(CH, HD), low(2 * CH, HD), low(2 * CH, HD),
         low(CH, HD), low(CH, HD),
@@ -597,7 +639,7 @@
         dma((2, 2, 4)), dma((2, 2, 4)),
         dma((2, 3)), dma((2, 3)),
         dma((2, 7)), dma((2, 7)),
-        dma((3,)), dma((3,)), dma((3,)), dma((3,)), dma((1,)), dma((1,)),
+        dma((3,)), dma((3,)), dma((4,)), dma((4,)),
         dma((2, 2, 4)), dma((2, 2, 4)),
         dma((4, 3)), dma((4, 3)),
         dma((2, 2)), dma((2, 2)), dma((8,)),
@@ -615,7 +657,7 @@
         compiler_params=pltpu.CompilerParams(
             collective_id=0, has_side_effects=True, vmem_limit_bytes=58 * 1024 * 1024),
     )(
-        doc_ids.reshape(1, TD), token_slot.reshape(1, TD), slot_image, cross_gate.reshape(1, WD),
+        doc_ids, token_slot, slot_image, cross_gate,
         query, key, value, cross_query, out_grad, latent_key, latent_value,
     )
     return pl.pallas_call(

time: 98.5 us -> 86.9 us (0.88)
  the two profiles are of different devices: /device:TPU:59 before, /device:TPU:53 now
where the time goes in v4:
time: 86.9 us; the launch traced here: 86.7 us
  Pallas kernels  86.1 us (99%)
    pallas_call x1, Pallas kernels, shards(): pl.pallas_call(kernel, out_shape=(half,) * 5 + (lat, lat), in_specs=[vm,...  83 us
    pallas_call x1, Pallas kernels, shards(): pl.pallas_call(widen, out_shape=(half,) + (full,) * 4 + (lat, lat), in_sp...  3.07 us

profile of v4, /device:TPU:53, one launch (start us, length us, event | category | flops | bytes accessed | tf_op | source)
XLA Modules:
  0.0 86.7 jit_solution(4586666966055831839)
XLA Ops:
  0.6 83.0 %shard_map.162 = (bf16[320,512]{1,0:T(8,128)(2,1)}, bf16[320,512]{1,0:T(8,128)(2,1)}, bf16[320,512]{1,0:T(8,128)(2,1)}, bf16[320,512]{1,0:T(8,128)(2,1)}, bf16[3...) custom-call(s32[320]{0:T(512)} %docs_ref.1, s32[320]{0:T(512)} %tok_ref.1, s32[4]{0:T(128)} %img_ref.1, ...), custom_call_target="tpu_custom_call" | custom-call | flops 6499999744 | bytes 8000000 | tf_op jit(solution)/shard_map/pallas_call | solution.py:650
  83.6 3.1 %shard_map.163 = (bf16[320,512]{1,0:T(8,128)(2,1)}, f32[320,512]{1,0:T(8,128)}, f32[320,512]{1,0:T(8,128)}, f32[320,512]{1,0:T(8,128)}, f32[320,512]{1,0:T(8,128...) custom-call(bf16[320,512]{1,0:T(8,128)(2,1)} %get-tuple-element.14.mixed_ref, ...), custom_call_target="tpu_custom_call" | custom-call | flops 1000000 | bytes 5000000 | tf_op jit(solution)/shard_map/pallas_call | solution.py:663

commit v5 on v4

--- a/solution.py
+++ b/solution.py
@@ -55,7 +55,7 @@
     obuf, dqb, part_k, part_v, own_k, own_v, got_k, got_v, sum_k, sum_v,
     o_in, dq_in, dk_in, dv_in,
     a_send, a_recv, z_send, z_recv, c_send, c_recv, l_send, l_recv, gx_send, gx_recv, gz_send, gz_recv,
-    p_send, p_recv, b_send, b_recv, f_send, f_recv, own_sem,
+    p_send, p_recv, b_send, b_recv, f_send, f_recv, own_sem, gates,
 ):
     s = lax.axis_index("seq")
     v = lax.axis_index("vis")
@@ -205,31 +205,38 @@
                 landed(stage.at[arr, i], f_recv.at[arr, i])
                 f_on(arr, i).start()
 
+    def z_sent(arr):
+        for dz in (1, 2):
+            @pl.when(z + dz < NX)
+            def _():
+                for i in range(NX):
+                    z_copy(arr, dz, i).wait_send()
+
     def z_wait(arr, dz):
         for i in range(NX):
             landed(bufs[arr].at[piece(2 - dz, xpeer(NX - ORDER[i])), :], z_recv.at[arr, dz - 1, i])
 
     def a_start(arr):
-        if arr < 2:
-            z_start(arr, 0)
         for d in ORDER[1:]:
             a_copy(arr, d).start()
 
     def a_finish(arr):
-        for i in range(1, NX):
-            a_wait(arr, ORDER[i])
-            if arr < 2:
-                z_start(arr, i)
+        for d in ORDER[1:]:
+            a_wait(arr, d)
+
+    def open_gate(n):
+        pl.semaphore_signal(gates.at[n], inc=1, device_id=(s, v + 1), device_id_type=MESH)
 
     @pl.when(core == 0)
     def _():
-        for arr in (0, 1, 2):
+        for arr in (0, 1):
+            z_start(arr, 0)
             a_start(arr)
 
     @pl.when(core == 1)
     def _():
-        for arr in (2, 3):
-            a_start(arr)
+        for arr in (0, 1):
+            z_start(arr, 0)
 
     for d in ORDER[1:]:
         c_copy(0, d).start()
@@ -247,20 +254,31 @@
 
     @pl.when(core == 0)
     def _():
-        a_finish(0)
-        a_finish(1)
+        for arr in (0, 1):
+            for i in range(1, NX):
+                a_wait(arr, ORDER[i])
+                z_start(arr, i)
+        open_gate(0)
+        a_start(2)
         a_start(3)
+        f_relay(0)
+        f_relay(1)
+        z_sent(0)
+        open_gate(1)
 
     @pl.when(core == 1)
     def _():
-        a_finish(2)
-        a_finish(3)
-        a_start(0)
-        a_start(1)
-        a_finish(0)
-        a_finish(1)
-
-    f_relay(0)
+        pl.semaphore_wait(gates.at[0], 1)
+        for arr in (0, 1):
+            a_start(arr)
+        for arr in (0, 1):
+            a_finish(arr)
+        a_start(2)
+        a_start(3)
+        pl.semaphore_wait(gates.at[1], 1)
+        for arr in (0, 1):
+            for i in range(1, NX):
+                z_start(arr, i)
 
     for d in ORDER[1:]:
         landed(cx.at[d - 1], c_recv.at[0, d - 1])
@@ -269,12 +287,7 @@
         c_copy(1, d).start()
     for i in range(8):
         own_copy(i).wait()
-    f_relay(1)
-
-    @pl.when(core == 0)
-    def _():
-        a_finish(2)
-
+    a_finish(2)
     for d in range(1, NX):
         landed(cz.at[d - 1], c_recv.at[1, d - 1])
     before = crow[...] + cz[0] + cz[1] + cz[2]
@@ -321,10 +334,12 @@
     dsum[1] = jnp.zeros((8, CH), F32)
     forward(2)
 
-    @pl.when(core == 0)
-    def _():
-        a_finish(3)
-
+    @pl.when(core == 1)
+    def _():
+        f_relay(0)
+        f_relay(1)
+
+    a_finish(3)
     dot_t[...] = dobuf[...].astype(F32).T
     row_sum(2)
 
@@ -573,15 +588,15 @@
         def _():
             gz_copy(j).wait_send()
 
+    @pl.when(core == 1)
+    def _():
+        z_sent(0)
+
+    z_sent(1)
     for arr in (0, 1):
         for d in range(1, IMAGES):
             l_copy(arr, d).wait_send()
         for dz in (1, 2):
-            @pl.when(z + dz < NX)
-            def _():
-                for i in range(NX):
-                    z_copy(arr, dz, i).wait_send()
-
             @pl.when(z >= dz)
             def _():
                 for p in range(NX):
@@ -642,7 +657,7 @@
         dma((3,)), dma((3,)), dma((4,)), dma((4,)),
         dma((2, 2, 4)), dma((2, 2, 4)),
         dma((4, 3)), dma((4, 3)),
-        dma((2, 2)), dma((2, 2)), dma((8,)),
+        dma((2, 2)), dma((2, 2)), dma((8,)), pltpu.SemaphoreType.REGULAR((2,)),
     ]
     full = jax.ShapeDtypeStruct((TD, WD), F32)
     half = jax.ShapeDtypeStruct((TD, WD), BF16)

time: 86.9 us -> 76.2 us (0.88)
  the two profiles are of different devices: /device:TPU:53 before, /device:TPU:59 now
where the time goes in v5:
time: 76.2 us; the launch traced here: 75.4 us
  Pallas kernels  74.8 us (98%)
    pallas_call x1, Pallas kernels, shards(): pl.pallas_call(kernel, out_shape=(half,) * 5 + (lat, lat), in_specs=[vm,...  71.7 us
    pallas_call x1, Pallas kernels, shards(): pl.pallas_call(widen, out_shape=(half,) + (full,) * 4 + (lat, lat), in_sp...  3.07 us

profile of v5, /device:TPU:59, one launch (start us, length us, event | category | flops | bytes accessed | tf_op | source)
XLA Modules:
  0.0 75.4 jit_solution(341852600248352750)
XLA Ops:
  0.6 71.7 %shard_map.162 = (bf16[320,512]{1,0:T(8,128)(2,1)}, bf16[320,512]{1,0:T(8,128)(2,1)}, bf16[320,512]{1,0:T(8,128)(2,1)}, bf16[320,512]{1,0:T(8,128)(2,1)}, bf16[3...) custom-call(s32[320]{0:T(512)} %docs_ref.1, s32[320]{0:T(512)} %tok_ref.1, s32[4]{0:T(128)} %img_ref.1, ...), custom_call_target="tpu_custom_call" | custom-call | flops 6499999744 | bytes 8000000 | tf_op jit(solution)/shard_map/pallas_call | solution.py:665
  72.3 3.1 %shard_map.163 = (bf16[320,512]{1,0:T(8,128)(2,1)}, f32[320,512]{1,0:T(8,128)}, f32[320,512]{1,0:T(8,128)}, f32[320,512]{1,0:T(8,128)}, f32[320,512]{1,0:T(8,128...) custom-call(bf16[320,512]{1,0:T(8,128)(2,1)} %get-tuple-element.14.mixed_ref, ...), custom_call_target="tpu_custom_call" | custom-call | flops 1000000 | bytes 5000000 | tf_op jit(solution)/shard_map/pallas_call | solution.py:678

commit v6 on v5

--- a/solution.py
+++ b/solution.py
@@ -53,9 +53,9 @@
     cown, cx, crow, cz, cqv, dov, stage,
     latk, latv, lks, lvs, gk, gv, cross, latsend, latx, latz, latin,
     obuf, dqb, part_k, part_v, own_k, own_v, got_k, got_v, sum_k, sum_v,
-    o_in, dq_in, dk_in, dv_in,
+    o_in, dq_in, dk_in, dv_in, mixed, cqg, lkg, lvg,
     a_send, a_recv, z_send, z_recv, c_send, c_recv, l_send, l_recv, gx_send, gx_recv, gz_send, gz_recv,
-    p_send, p_recv, b_send, b_recv, f_send, f_recv, own_sem, gates,
+    p_send, p_recv, b_send, b_recv, f_send, f_recv, own_sem, out_sem, gates,
 ):
     s = lax.axis_index("seq")
     v = lax.axis_index("vis")
@@ -133,6 +133,13 @@
         )[i]
         return pltpu.make_async_copy(src, dst, own_sem.at[i])
 
+    def out_copy(i):
+        src, dst = (
+            (mixed, mixed_ref), (dq_in, qg_ref), (dk_in, kg_ref), (dv_in, vg_ref), (cqg, cqg_ref),
+            (lkg, lkg_ref.at[0]), (lvg, lvg_ref.at[0]),
+        )[i]
+        return pltpu.make_async_copy(src, dst, out_sem.at[i])
+
     for i in range(8):
         own_copy(i).start()
 
@@ -287,7 +294,6 @@
         c_copy(1, d).start()
     for i in range(8):
         own_copy(i).wait()
-    a_finish(2)
     for d in range(1, NX):
         landed(cz.at[d - 1], c_recv.at[1, d - 1])
     before = crow[...] + cz[0] + cz[1] + cz[2]
@@ -326,22 +332,6 @@
             pbuf[at + k0:at + k0 + kn, across] = pb
             sums[slot, :, across] += fold(p, jnp.sum)
             opart[slot, :, across] += dot(vt[:, at + k0:at + k0 + kn], pb)
-
-    def row_sum(slot):
-        dsum[slot] = jnp.broadcast_to(jnp.sum(dot_t[...] * opart[slot], axis=0, keepdims=True), (8, CH))
-
-    dsum[0] = jnp.zeros((8, CH), F32)
-    dsum[1] = jnp.zeros((8, CH), F32)
-    forward(2)
-
-    @pl.when(core == 1)
-    def _():
-        f_relay(0)
-        f_relay(1)
-
-    a_finish(3)
-    dot_t[...] = dobuf[...].astype(F32).T
-    row_sum(2)
 
     for arr in (0, 1):
         for d in range(1, IMAGES):
@@ -368,9 +358,11 @@
         gp = dot(lvh, back, NT)
         cdot = jnp.sum(probs * gp, axis=0, keepdims=True)
         ds = (probs * (gp - cdot) * SCALE).astype(BF16)
-        cqg_ref[:, sl] = dot(lkh.T, ds).T.astype(cqg_ref.dtype)
+        cqg[:, sl] = dot(lkh.T, ds).T.astype(BF16)
         gk[:, sl] = dot(ds, cqh).astype(BF16).astype(F32)
         gv[:, sl] = dot(low, back).astype(BF16).astype(F32)
+
+    out_copy(4).start()
 
     for m in range(IMAGES):
         for n, g in enumerate((gk, gv)):
@@ -391,6 +383,23 @@
 
     for d in ORDER[1:]:
         gx_copy(d).start()
+
+    def row_sum(slot):
+        dsum[slot] = jnp.broadcast_to(jnp.sum(dot_t[...] * opart[slot], axis=0, keepdims=True), (8, CH))
+
+    dsum[0] = jnp.zeros((8, CH), F32)
+    dsum[1] = jnp.zeros((8, CH), F32)
+
+    @pl.when(core == 1)
+    def _():
+        f_relay(0)
+        f_relay(1)
+
+    a_finish(2)
+    forward(2)
+    a_finish(3)
+    dot_t[...] = dobuf[...].astype(F32).T
+    row_sum(2)
 
     @pl.when(z >= 1)
     def _():
@@ -553,28 +562,32 @@
 
     for d in ORDER[1:]:
         b_wait(0, d)
-    mixed_ref[...] = (o_in[...].astype(F32) + cross[...]).astype(BF16)
+    mixed[...] = (o_in[...].astype(F32) + cross[...]).astype(BF16)
+    out_copy(0).start()
 
     for i in range(NX):
         @pl.when(jnp.logical_not(from_self(i)))
         def _():
             landed(latin.at[i], gz_recv.at[i])
 
-    for n, g in enumerate((lkg_ref, lvg_ref)):
+    for n, g in enumerate((lkg, lvg)):
         acc = latin[0, n].astype(F32)
         for i in range(1, NX):
             acc = acc + latin[i, n].astype(F32)
-        g[0] = acc
+        g[...] = acc
+        out_copy(5 + n).start()
     for d in ORDER[1:]:
         b_wait(1, d)
-    qg_ref[...] = dq_in[...]
-
-    for arr, out_ in ((2, kg_ref), (3, vg_ref)):
+    out_copy(1).start()
+
+    for arr in (2, 3):
         b_own(arr)
         for d in ORDER[1:]:
             b_wait(arr, d)
-        out_[...] = backs[arr][...]
-
+        out_copy(arr).start()
+
+    for i in range(7):
+        out_copy(i).wait()
     for d in range(1, NX):
         for arr in range(4):
             a_copy(arr, d).wait_send()
@@ -613,11 +626,26 @@
                 r_on(arr, p).wait_send()
 
 
-def widen(mixed_ref, *refs):
-    half = len(refs) // 2
-    refs[half][...] = mixed_ref[...]
-    for src, dst in zip(refs[:half], refs[half + 1:]):
-        dst[...] = src[...].astype(F32)
+def widen(*refs):
+    ins, outs, (narrow, full, lat, in_sem, out_sem) = refs[:7], refs[7:14], refs[14:]
+
+    def fetch(i):
+        dst = narrow.at[i] if i < 5 else lat.at[i - 5]
+        return pltpu.make_async_copy(ins[i], dst, in_sem.at[i])
+
+    def keep(i):
+        src = narrow.at[0] if i == 0 else full.at[i - 1] if i < 5 else lat.at[i - 5]
+        return pltpu.make_async_copy(src, outs[i], out_sem.at[i])
+
+    for i in range(7):
+        fetch(i).start()
+    for i in range(7):
+        fetch(i).wait()
+        if 1 <= i <= 4:
+            full[i - 1] = narrow[i].astype(F32)
+        keep(i).start()
+    for i in range(7):
+        keep(i).wait()
 
 
 def shards(query, key, value, doc_ids, cross_query, latent_key, latent_value, token_slot,
@@ -650,6 +678,7 @@
         wide(CH, HD), wide(CH, HD), low(2 * CH, HD), low(2 * CH, HD),
         low(CH, HD), low(CH, HD),
         low(TD, WD), low(TD, WD), low(TD, WD), low(TD, WD),
+        low(TD, WD), low(TD, WD), wide(LAT, 256), wide(LAT, 256),
         dma((4, 3)), dma((4, 3)),
         dma((2, 2, 4)), dma((2, 2, 4)),
         dma((2, 3)), dma((2, 3)),
@@ -657,7 +686,7 @@
         dma((3,)), dma((3,)), dma((4,)), dma((4,)),
         dma((2, 2, 4)), dma((2, 2, 4)),
         dma((4, 3)), dma((4, 3)),
-        dma((2, 2)), dma((2, 2)), dma((8,)), pltpu.SemaphoreType.REGULAR((2,)),
+        dma((2, 2)), dma((2, 2)), dma((8,)), dma((7,)), pltpu.SemaphoreType.REGULAR((2,)),
     ]
     full = jax.ShapeDtypeStruct((TD, WD), F32)
     half = jax.ShapeDtypeStruct((TD, WD), BF16)
@@ -666,7 +695,7 @@
         kernel,
         out_shape=(half,) * 5 + (lat, lat),
         in_specs=[vm, vm, sm, vm] + [hbm] * 7,
-        out_specs=(vm,) * 7,
+        out_specs=(hbm,) * 7,
         scratch_shapes=scratch,
         cost_estimate=pl.CostEstimate(flops=6_500_000_000, bytes_accessed=8_000_000, transcendentals=4_000_000),
         compiler_params=pltpu.CompilerParams(
@@ -678,8 +707,9 @@
     return pl.pallas_call(
         widen,
         out_shape=(half,) + (full,) * 4 + (lat, lat),
-        in_specs=[vm] * 7,
-        out_specs=(vm,) * 7,
+        in_specs=[hbm] * 7,
+        out_specs=(hbm,) * 7,
+        scratch_shapes=[low(5, TD, WD), wide(4, TD, WD), wide(2, 1, LAT, 256), dma((7,)), dma((7,))],
         cost_estimate=pl.CostEstimate(flops=1_000_000, bytes_accessed=5_000_000, transcendentals=0),
     )(*results)
 

time: 76.2 us -> 74.7 us (0.980)
  Pallas kernels: 74.8 us -> 73.5 us
    pallas_call x1, Pallas kernels: 71.7 us -> 70.7 us  [shards(): pl.pallas_call(kernel, out_shape=(half,) * 5 + (lat, lat), in_specs=[vm,...]
where the time goes in v6:
time: 74.7 us; the launch traced here: 74.3 us
  Pallas kernels  73.5 us (98%)
  between operations  0.81 us (1%)
    pallas_call x1, Pallas kernels, shards(): pl.pallas_call(kernel, out_shape=(half,) * 5 + (lat, lat), in_specs=[vm,...  70.7 us
    pallas_call x1, Pallas kernels, shards(): pl.pallas_call(widen, out_shape=(half,) + (full,) * 4 + (lat, lat), in_sp...  2.75 us

profile of v6, /device:TPU:59, one launch (start us, length us, event | category | flops | bytes accessed | tf_op | source)
XLA Modules:
  0.0 74.3 jit_solution(15097518142969271958)
XLA Ops:
  0.6 70.7 %shard_map.162 = (bf16[320,512]{1,0:T(8,128)(2,1)}, bf16[320,512]{1,0:T(8,128)(2,1)}, bf16[320,512]{1,0:T(8,128)(2,1)}, bf16[320,512]{1,0:T(8,128)(2,1)}, bf16[3...) custom-call(s32[320]{0:T(512)} %docs_ref.1, s32[320]{0:T(512)} %tok_ref.1, s32[4]{0:T(128)} %img_ref.1, ...), custom_call_target="tpu_custom_call" | custom-call | flops 6499999744 | bytes 8000000 | tf_op jit(solution)/shard_map/pallas_call | solution.py:694
  71.4 2.8 %shard_map.163 = (bf16[320,512]{1,0:T(8,128)(2,1)}, f32[320,512]{1,0:T(8,128)}, f32[320,512]{1,0:T(8,128)}, f32[320,512]{1,0:T(8,128)}, f32[320,512]{1,0:T(8,128...) custom-call(bf16[320,512]{1,0:T(8,128)(2,1)} %get-tuple-element.14.refs_0_, bf16[320,512]{1,0:T(8,128)(2,1)} %get-tuple-element.15.refs_1_, ...), custom_call_target="tpu_custom_call" | custom-call | flops 1000000 | bytes 5000000 | tf_op jit(solution)/shard_map/pallas_call | solution.py:707

commit v7 on v6

--- a/solution.py
+++ b/solution.py
@@ -448,8 +448,8 @@
     parts, gots = (part_k, part_v), (got_k, got_v)
 
     def p_copy(arr, dz, p):
-        return remote(parts[arr].at[pl.ds((2 - dz) * CH + p * TD, TD), :],
-                      gots[arr].at[pl.ds((dz - 1) * CH + p * TD, TD), :],
+        return remote(parts[arr].at[piece(2 - dz, p), :],
+                      gots[arr].at[piece(dz - 1, p), :],
                       p_send.at[arr, dz - 1, p], p_recv.at[arr, dz - 1, p], s - dz * NX, v)
 
     def r_copy(arr, p):
@@ -473,12 +473,18 @@
             else:
                 p_copy(arr, dz, p).start()
 
+    def turn(j):
+        return (x, x + 1 - 2 * lax.rem(x, 2), lax.rem(x + 2, NX), NX - 1 - x)[j]
+
     def backward(slot):
         at = slot * CH
         sent = 0
         dol[slot] = (dot_t[...] * maxes[slot, 0:1, :]).T.astype(BF16)
         for k0, kn, q0, qn in BWD_TILES[slot]:
             down, across = slice(at + k0, at + k0 + kn), slice(q0, q0 + qn)
+            if slot == 1:
+                first = lax.rem(lax.div(x, 2) + k0 // kn, 2)
+                down = pl.ds(pl.multiple_of(at + first * kn, 128), kn)
             pb = pbuf[down, across]
             grad = dol[slot, across, :]
             dp = dot(vbuf[down, :], grad, NT)
@@ -493,7 +499,7 @@
                 part_k[down, :] = dk.astype(BF16)
                 part_v[down, :] = dv.astype(BF16)
                 while (sent + 1) * TD <= k0 + kn:
-                    p_start(2 - slot, sent)
+                    p_start(2 - slot, turn(sent) if slot == 1 else sent)
                     sent += 1
 
     @pl.when(z >= 2)
@@ -540,12 +546,13 @@
                 r_on(arr, p).start()
 
     def p_wait(arr, dz, p):
-        here = gots[arr].at[pl.ds((dz - 1) * CH + p * TD, TD), :]
+        here = gots[arr].at[piece(dz - 1, p), :]
         landed(here, p_recv.at[arr, dz - 1, p])
         return here
 
-    for p in range(NX):
-        sl = slice(p * TD, (p + 1) * TD)
+    for j in range(NX):
+        p = turn(j)
+        sl = rows(p)
         for arr, (own, out_) in enumerate(((own_k, sum_k), (own_v, sum_v))):
             for dz in (2, 1):
                 @pl.when(z + dz < NX)
@@ -553,9 +560,7 @@
                     here = p_wait(arr, dz, p)
                     own[sl, :] += here[...].astype(F32)
             out_[sl, :] = own[sl, :].astype(BF16)
-
-            @pl.when(x != p)
-            def _():
+            if j:
                 d = lax.rem(p - x + NX, NX)
                 remote(out_.at[sl, :], backs[arr + 2].at[:, cols(x)],
                        b_send.at[arr + 2, d - 1], b_recv.at[arr + 2, d - 1], z * NX + p, v).start()

time: 74.7 us -> 75.8 us (1.015)
  no operation moved by 1% of the time
where the time goes in v7:
time: 75.8 us; the launch traced here: 74.7 us
  Pallas kernels  73.9 us (97%)
  between operations  0.81 us (1%)
    pallas_call x1, Pallas kernels, shards(): pl.pallas_call(kernel, out_shape=(half,) * 5 + (lat, lat), in_specs=[vm,...  71.1 us
    pallas_call x1, Pallas kernels, shards(): pl.pallas_call(widen, out_shape=(half,) + (full,) * 4 + (lat, lat), in_sp...  2.75 us

profile of v7, /device:TPU:59, one launch (start us, length us, event | category | flops | bytes accessed | tf_op | source)
XLA Modules:
  0.0 74.7 jit_solution(4641093989629720861)
XLA Ops:
  0.6 71.1 %shard_map.162 = (bf16[320,512]{1,0:T(8,128)(2,1)}, bf16[320,512]{1,0:T(8,128)(2,1)}, bf16[320,512]{1,0:T(8,128)(2,1)}, bf16[320,512]{1,0:T(8,128)(2,1)}, bf16[3...) custom-call(s32[320]{0:T(512)} %docs_ref.1, s32[320]{0:T(512)} %tok_ref.1, s32[4]{0:T(128)} %img_ref.1, ...), custom_call_target="tpu_custom_call" | custom-call | flops 6499999744 | bytes 8000000 | tf_op jit(solution)/shard_map/pallas_call | solution.py:699
  71.8 2.8 %shard_map.163 = (bf16[320,512]{1,0:T(8,128)(2,1)}, f32[320,512]{1,0:T(8,128)}, f32[320,512]{1,0:T(8,128)}, f32[320,512]{1,0:T(8,128)}, f32[320,512]{1,0:T(8,128...) custom-call(bf16[320,512]{1,0:T(8,128)(2,1)} %get-tuple-element.14.refs_0_, bf16[320,512]{1,0:T(8,128)(2,1)} %get-tuple-element.15.refs_1_, ...), custom_call_target="tpu_custom_call" | custom-call | flops 1000000 | bytes 5000000 | tf_op jit(solution)/shard_map/pallas_call | solution.py:712

commit v8 on v6

--- a/solution.py
+++ b/solution.py
@@ -188,6 +188,10 @@
                       f_send.at[arr, i], z_recv.at[arr, 1, i], s - NX, v)
 
     def z_start(arr, i):
+        @pl.when(z <= 2)
+        def _():
+            z_copy(arr, 1, i).start()
+
         if i < 2:
             @pl.when(z == 0)
             def _():
@@ -201,10 +205,6 @@
             def _():
                 z_copy(arr, 2, i).start()
 
-        @pl.when(z <= 2)
-        def _():
-            z_copy(arr, 1, i).start()
-
     def f_relay(arr):
         @pl.when(z == 3)
         def _():
@@ -266,12 +266,12 @@
                 a_wait(arr, ORDER[i])
                 z_start(arr, i)
         open_gate(0)
+        open_gate(1)
         a_start(2)
         a_start(3)
         f_relay(0)
         f_relay(1)
         z_sent(0)
-        open_gate(1)
 
     @pl.when(core == 1)
     def _():

time: 74.7 us -> 74.7 us (level)
  no operation moved by 1% of the time
where the time goes in v8:
time: 74.7 us; the launch traced here: 74.3 us
  Pallas kernels  73.5 us (98%)
  between operations  0.81 us (1%)
    pallas_call x1, Pallas kernels, shards(): pl.pallas_call(kernel, out_shape=(half,) * 5 + (lat, lat), in_specs=[vm,...  70.7 us
    pallas_call x1, Pallas kernels, shards(): pl.pallas_call(widen, out_shape=(half,) + (full,) * 4 + (lat, lat), in_sp...  2.75 us

profile of v8, /device:TPU:59, one launch (start us, length us, event | category | flops | bytes accessed | tf_op | source)
XLA Modules:
  0.0 74.3 jit_solution(2867345286516878743)
XLA Ops:
  0.6 70.7 %shard_map.162 = (bf16[320,512]{1,0:T(8,128)(2,1)}, bf16[320,512]{1,0:T(8,128)(2,1)}, bf16[320,512]{1,0:T(8,128)(2,1)}, bf16[320,512]{1,0:T(8,128)(2,1)}, bf16[3...) custom-call(s32[320]{0:T(512)} %docs_ref.1, s32[320]{0:T(512)} %tok_ref.1, s32[4]{0:T(128)} %img_ref.1, ...), custom_call_target="tpu_custom_call" | custom-call | flops 6499999744 | bytes 8000000 | tf_op jit(solution)/shard_map/pallas_call | solution.py:694
  71.4 2.8 %shard_map.163 = (bf16[320,512]{1,0:T(8,128)(2,1)}, f32[320,512]{1,0:T(8,128)}, f32[320,512]{1,0:T(8,128)}, f32[320,512]{1,0:T(8,128)}, f32[320,512]{1,0:T(8,128...) custom-call(bf16[320,512]{1,0:T(8,128)(2,1)} %get-tuple-element.14.refs_0_, bf16[320,512]{1,0:T(8,128)(2,1)} %get-tuple-element.15.refs_1_, ...), custom_call_target="tpu_custom_call" | custom-call | flops 1000000 | bytes 5000000 | tf_op jit(solution)/shard_map/pallas_call | solution.py:707
